TPU v7x, 32 devices: a whole 2x2x4 slice. The times are simulated.
32 devices in a mesh: dp: 8 (over z, x), mp: 4 (over y, core).
Axes of the slice: x: 2, y: 2, z: 4, core: 2. Of those that a mesh axis runs over, the one named last changes fastest.
Arguments:
- inputs: bfloat16 [8192, 768], P('dp'), may hold values from -6 to 6
- page_feat: bfloat16 [8, 8, 768], P('dp'), may hold values from -6 to 6
- page_onehot: int32 [8192, 8], P('dp'), may hold values from 0 to 1, as said below
- lengths: int32 [8], P('dp'), may hold values from 256 to 1024, as said below
- hor_pos: int32 [8192], P('dp'), may hold values from 0 to 999
- ver_pos: int32 [8192], P('dp'), may hold values from 0 to 999
- norm1_gain: bfloat16 [768], replicated, may hold values from 0.099609375 to 1.8984375
- w_query: bfloat16 [768, 768], P(None, 'mp'), may hold values from -0.21875 to 0.21875
- w_key: bfloat16 [768, 768], P(None, 'mp'), may hold values from -0.21875 to 0.21875
- w_value: bfloat16 [768, 768], P(None, 'mp'), may hold values from -0.21875 to 0.21875
- rel_table: bfloat16 [12, 32], P('mp'), may hold values from -4 to 4
- hor_table: bfloat16 [12, 32], P('mp'), may hold values from -4 to 4
- ver_table: bfloat16 [12, 32], P('mp'), may hold values from -4 to 4
- w_output: bfloat16 [768, 768], P('mp'), may hold values from -0.875 to 0.875
- norm2_gain: bfloat16 [768], replicated, may hold values from 0.099609375 to 1.8984375
- w_up: bfloat16 [768, 3072], P(None, 'mp'), may hold values from -0.21875 to 0.21875
- w_down: bfloat16 [3072, 768], P('mp'), may hold values from -0.15625 to 0.15625
- cotangent: bfloat16 [8192, 768], P('dp'), may hold values from -6 to 6
Outputs:
- output: bfloat16 [8192, 768], P('dp')
- grad_inputs: float32 [8192, 768], P('dp')
- grad_page_feat: float32 [8, 8, 768], P('dp')
- grad_norm1_gain: float32 [768], P('dp')
- grad_w_query: float32 [768, 768], P('dp', 'mp')
- grad_w_key: float32 [768, 768], P('dp', 'mp')
- grad_w_value: float32 [768, 768], P('dp', 'mp')
- grad_rel_table: float32 [12, 32], P('mp')
- grad_hor_table: float32 [12, 32], P('mp')
- grad_ver_table: float32 [12, 32], P('mp')
- grad_w_output: float32 [768, 768], P('mp', 'dp')
- grad_norm2_gain: float32 [768], P('dp')
- grad_w_up: float32 [768, 3072], P('dp', 'mp')
- grad_w_down: float32 [3072, 768], P('mp', 'dp')
Inputs may be any that keep to these rules, and one draw needn't show every extreme that they name: `lengths`: keys at or past a sequence's length are padding; in every draw some sequence uses all 1024 slots. `page_onehot`: each row has exactly one 1; within a sequence the page number never falls from one token to the next.
All inputs are finite; a program needn't handle non-finite values.
Results may differ from a plain program's by a relative error of at most 0.012.
Values may be sent and summed in bfloat16 or wider, within the bound.
No kernel may reach another device: no remote copies, remote signals or barrier semaphores. Data moves between devices by JAX's collectives and lax.ppermute only.
A program may use at most 192 MiB of HBM per device.

v0:
```python
import functools

import jax
import jax.numpy as jnp
import numpy as np
from jax import lax
from jax.experimental import pallas as pl
from jax.experimental.pallas import tpu as pltpu
from jax.sharding import PartitionSpec as P

EPS = 1e-06
THRESHOLDS = (12, 16, 23, 32, 46, 64, 91)
FAR = 91
HEADS = 3
HD = 64
PAD = 128
MARKS = 72
NEAR = 40
TILES = NEAR + 2
SPAN = 384
LOW = 92
TOP = 311
BF = jnp.bfloat16
F32 = jnp.float32
I32 = jnp.int32
FEED_CHUNK = 256
PLACES = 1024
TABLES_MIB = 18
GELU_C = float(np.sqrt(2.0 / np.pi))


def dot(left, right, dims=((1,), (0,))):
    return lax.dot_general(left, right, (dims, ((), ())), preferred_element_type=F32)


def bucket(delta):
    magnitude = jnp.abs(delta)
    coarse = 8 + sum((magnitude >= limit).astype(I32) for limit in THRESHOLDS)
    return jnp.where(magnitude < 8, magnitude, coarse) + 16 * (delta > 0).astype(I32)


def params(mib):
    return pltpu.CompilerParams(vmem_limit_bytes=mib * 2**20)


def cost(microseconds):
    return pl.CostEstimate(flops=int(1.15e9 * microseconds), bytes_accessed=1, transcendentals=0)


def shape(dims, dtype):
    return jax.ShapeDtypeStruct(dims, dtype)


def whole(dims):
    return pl.BlockSpec(dims, lambda *a: (0,) * len(dims))


VMEM = pl.BlockSpec(memory_space=pltpu.VMEM)


def call(kernel, name, ids, arrays, outs, *, mib, us, scratch=()):
    return pl.pallas_call(
        kernel,
        grid_spec=pltpu.PrefetchScalarGridSpec(
            num_scalar_prefetch=1,
            grid=(1,),
            in_specs=[VMEM] * len(arrays),
            out_specs=jax.tree.map(lambda _: VMEM, outs),
            scratch_shapes=list(scratch),
        ),
        out_shape=outs,
        compiler_params=params(mib),
        cost_estimate=cost(us),
        name=name,
    )(ids, *arrays)


def quarter_of(place, size):
    return pl.ds(pl.multiple_of(place * size, 128), size)


def hidden_rows(inputs, pages, feats):
    return inputs.astype(F32) + dot(pages.astype(F32).astype(BF), feats, ((0,), (0,)))


def unit_rows(field):
    factor = lax.rsqrt(jnp.mean(field * field, axis=-1, keepdims=True) + EPS)
    return field * factor, factor


def project_kernel(ids, x_ref, page_ref, feat_ref, gain_ref, wq_ref, wk_ref, wv_ref, n_ref, q_ref, k_ref, v_ref):
    rows = 256

    def block_of(step, carry):
        here = quarter_of(step, rows)
        unit, _ = unit_rows(hidden_rows(x_ref[here, :], page_ref[:, here], feat_ref[...]))
        normed = (unit * gain_ref[...].astype(F32).reshape(1, -1)).astype(BF)
        n_ref[here, :] = normed
        lane = lax.broadcasted_iota(I32, (rows, PAD), 1)
        row = lax.broadcasted_iota(I32, (rows, PAD), 0) + step * rows
        masked = jnp.where((lane == HD) & (row >= ids[8]), -1e30, 0.0)
        block = lane - MARKS
        far_left = (block >= 0) & (block < 8) & (row < 128 * block - 96)
        far_right = (block >= 8) & (block < 16) & (row >= 128 * (block - 8) + 224)
        masked = jnp.where(far_left | far_right, 1.0, masked)
        query_extra = jnp.where(lane == HD, 1.0, 0.0)
        value_extra = jnp.where((lane == HD) | (lane == HD + 1), 1.0, 0.0)
        for out_ref, w_ref, extra, scale in (
            (q_ref, wq_ref, query_extra, 0.125),
            (k_ref, wk_ref, masked, None),
            (v_ref, wv_ref, value_extra, None),
        ):
            full = dot(normed, w_ref[...], ((1,), (1,)))
            if scale is not None:
                full = full * scale
            pair = full[:, :PAD]
            last = jnp.concatenate([full[:, PAD:], jnp.zeros((rows, PAD - HD), F32)], axis=1)
            heads = (pair, pltpu.roll(pair, HD, 1), last)
            for head in range(HEADS):
                out_ref[here, head * PAD : (head + 1) * PAD] = jnp.where(lane < HD, heads[head], extra).astype(BF)
        return carry

    lax.fori_loop(0, x_ref.shape[0] // rows, block_of, 0)


def project(ids, *arrays):
    seq, width = arrays[0].shape
    outs = [shape((seq, width), BF)] + [shape((seq, HEADS * PAD), BF)] * 3
    return call(project_kernel, "project", ids, arrays, outs, mib=16, us=7)


def place(delta):
    magnitude = jnp.abs(delta)
    coarse = jnp.minimum(25 - lax.clz(delta * delta), 7)
    exact = magnitude < 8
    return jnp.where(exact, magnitude, coarse), exact, delta > 0


def look(table_ref, row, where):
    index, exact, after = where
    found = [jnp.take_along_axis(table_ref[row, part], index, axis=0) for part in range(4)]
    return jnp.where(after, jnp.where(exact, found[2], found[3]), jnp.where(exact, found[0], found[1]))


def tile_delta(tile):
    lane = lax.broadcasted_iota(I32, (8, 128), 1)
    sub = lax.broadcasted_iota(I32, (8, 128), 0)
    delta = 8 * (tile - 13) + sub - lane
    if tile == 0:
        delta = jnp.full_like(delta, -1000)
    if tile == TILES - 1:
        delta = jnp.full_like(delta, 1000)
    return delta


def attend_kernel(*refs, first, chunk):
    ids, q_ref, k_ref, v_ref, hor_ref, ver_ref = refs[:6]
    if first:
        hor_all, ver_all, rel_table, hor_table, ver_table, e_ref, att0, att1, inv_ref, out_ref = refs[6:16]
        rel_ref, t8_ref, hor_col, ver_col, s_ref = refs[16:]
    else:
        rel_ref, t8_ref, hor_col, ver_col, e_ref, att0, att1, inv_ref, out_ref, s_ref = refs[6:]
    seq = k_ref.shape[0]
    width = seq // 4
    lanes = width // 128

    if first:
        for all_ref, col_ref in ((hor_all, hor_col), (ver_all, ver_col)):
            for b in range(seq // 128):
                cols = slice(128 * b, 128 * b + 128)
                spread = jnp.broadcast_to(all_ref[:, cols].astype(F32), (128, 128))
                col_ref[cols, :] = spread.T.astype(I32)
        lane = lax.broadcasted_iota(I32, (8, 32), 1)
        sub = lax.broadcasted_iota(I32, (8, 32), 0)
        for axis, table_ref in enumerate((rel_table, hor_table, ver_table)):
            table = table_ref[...].astype(F32)
            for head in range(HEADS):
                row = jnp.broadcast_to(table[head : head + 1], (8, 32))
                for part in range(4):
                    entries = jnp.sum(jnp.where(lane == sub + 8 * part, row, 0.0), axis=1, keepdims=True)
                    t8_ref[axis * HEADS + head, part] = jnp.broadcast_to(entries, (8, 128))
        for tile in range(TILES):
            where = place(tile_delta(tile))
            for head in range(HEADS):
                rel_ref[head, tile] = look(t8_ref, head, where)

    def products(here):
        queries = q_ref[here, :]
        for head in range(HEADS):
            cols = slice(head * PAD, (head + 1) * PAD)
            s_ref[head] = dot(k_ref[:, cols], queries[:, cols], ((1,), (1,)))

    def biases(place_of, here):
        hor_row, ver_row = hor_ref[:, here], ver_ref[:, here]
        hor = [jnp.broadcast_to(hor_row[:, 128 * l : 128 * l + 128], (8, 128)) for l in range(lanes)]
        ver = [jnp.broadcast_to(ver_row[:, 128 * l : 128 * l + 128], (8, 128)) for l in range(lanes)]
        block = place_of * lanes

        def add_bias(c, tops):
            tops = list(tops)
            base = pl.multiple_of(c * chunk, chunk)
            for g in range(chunk // 8):
                rows = pl.ds(pl.multiple_of(base + 8 * g, 8), 8)
                hor_keys, ver_keys = hor_col[rows, :], ver_col[rows, :]
                for l in range(lanes):
                    cols = pl.ds(128 * l, 128)
                    hor_at, ver_at = place(hor_keys - hor[l]), place(ver_keys - ver[l])
                    tile = jnp.clip(c * (chunk // 8) + g - 16 * (block + l) + 13, 0, TILES - 1)
                    for head in range(HEADS):
                        s = s_ref[head, rows, cols] + rel_ref[head, tile]
                        s = s + (look(t8_ref, HEADS + head, hor_at) + look(t8_ref, 2 * HEADS + head, ver_at))
                        s_ref[head, rows, cols] = s
                        tops[head * lanes + l] = jnp.maximum(tops[head * lanes + l], s)
            return tuple(tops)

        tops = lax.fori_loop(
            0, seq // chunk, add_bias, tuple(jnp.full((8, 128), -1e30, F32) for _ in range(HEADS * lanes))
        )
        return [jnp.broadcast_to(jnp.max(top, axis=0, keepdims=True), (16, 128)) for top in tops]

    def attended(part, peaks):
        mine = quarter_of(part, width)
        for head in range(HEADS):
            for g in range(seq // 16):
                rows = slice(16 * g, 16 * g + 16)
                for l in range(lanes):
                    cols = slice(128 * l, 128 * l + 128)
                    into = pl.ds(pl.multiple_of(part * width + 128 * l, 128), 128)
                    e_ref[head, rows, into] = jnp.exp(s_ref[head, rows, cols] - peaks[head * lanes + l]).astype(BF)
            total = dot(v_ref[:, head * PAD : (head + 1) * PAD], e_ref[head, :, mine], ((0,), (0,)))
            inverse = 1.0 / total[HD : HD + 1, :]
            inv_ref[head : head + 1, mine] = inverse
            out_ref[head * HD : (head + 1) * HD, mine] = total[:HD] * inverse
        for at, att_ref in enumerate((att0, att1)):

            @pl.when(part == at)
            def _(att_ref=att_ref):
                att_ref[...] = out_ref[:, mine].astype(BF)

    def quarter(part, carry):
        place_of = ids[(0 if first else 2) + part]
        here = quarter_of(place_of, width)
        products(here)
        attended(part, biases(place_of, here))
        return carry

    lax.fori_loop(0, 2, quarter, 0)


def attend(ids, queries, keys, values, hor, ver, tables, lookups):
    seq = queries.shape[0]
    width = seq // 4
    first = lookups is None
    columns = HEADS * HD
    made = [
        shape((HEADS, TILES, 8, 128), F32), shape((3 * HEADS, 4, 8, 128), F32), shape((seq, 128), I32), shape((seq, 128), I32)
    ]
    extra = (hor, ver, *tables) if first else tuple(lookups)
    outs = [
        shape((HEADS, seq, 2 * width), BF), shape((columns, width), BF), shape((columns, width), BF),
        shape((HEADS, 2 * width), F32), shape((columns, 2 * width), F32),
    ]
    found = call(
        functools.partial(attend_kernel, first=first, chunk=128),
        "attend_first" if first else "attend_last",
        ids,
        (queries, keys, values, hor, ver, *extra),
        outs + made if first else outs,
        mib=14,
        us=14,
        scratch=[pltpu.VMEM((HEADS, seq, width), F32)],
    )
    return found[:5], found[5:]


def feed_kernel(
    ids, x_ref, page_ref, feat_ref, gain_ref, cot_ref, a0, a1, a2, a3, o0, o1, o2, o3, u0, u1, d0, d1,
    keep_ref, send_ref, mixed_ref, grad_ref, ffn_ref, *, slot,
):
    here = quarter_of(ids[slot], mixed_ref.shape[0])
    cotangent = cot_ref[here, :]
    mixed = hidden_rows(x_ref[here, :], page_ref[:, here], feat_ref[...])
    for a_ref, o_ref in ((a0, o0), (a1, o1), (a2, o2), (a3, o3)):
        mixed = mixed + dot(a_ref[...], o_ref[...], ((0,), (0,)))
    mixed_ref[...] = mixed
    unit, _ = unit_rows(mixed)
    normed = (unit * gain_ref[...].astype(F32).reshape(1, -1)).astype(BF)
    send_ref[2] = normed
    units = u0.shape[1]
    for u_ref, d_ref, goal in ((u0, d0, keep_ref), (u1, d1, send_ref)):
        for at in range(0, units, FEED_CHUNK):
            cols = slice(at, at + FEED_CHUNK)
            upward = dot(normed, u_ref[:, cols])
            square = upward * upward
            tanh = jnp.tanh(GELU_C * upward * (1.0 + 0.044715 * square))
            lifted = 0.5 * (1.0 + tanh)
            activated = (upward * lifted).astype(BF)
            slope = lifted + 0.5 * upward * (1.0 - tanh * tanh) * (GELU_C * (1.0 + 3 * 0.044715 * square))
            grad_up = (dot(cotangent, d_ref[cols, :], ((1,), (1,))) * slope).astype(BF)
            goal[0, :, cols] = activated
            goal[1, :, cols] = grad_up
    ffn = dot(keep_ref[0], d0[...]) + dot(send_ref[0], d1[...])
    ffn_ref[...] = ffn.astype(ffn_ref.dtype)
    grad = dot(keep_ref[1], u0[...], ((1,), (1,))) + dot(send_ref[1], u1[...], ((1,), (1,)))
    grad_ref[...] = grad.astype(grad_ref.dtype)


def feed(ids, own, inputs, onehot, feats, gain, cotangent, attended, w_outputs, ups, downs):
    seq, width = inputs.shape
    rows = seq // 4
    units = ups[0].shape[1]
    kept = F32 if own else BF
    outs = [
        shape((2, rows, units), BF), shape((3, rows, width), BF), shape((rows, width), F32),
        shape((rows, width), BF), shape((rows, width), kept),
    ]
    return call(
        functools.partial(feed_kernel, slot=0 if own else 2),
        "feed_own" if own else "feed_other",
        ids,
        (inputs, onehot, feats, gain, cotangent, *attended, *w_outputs, *ups, *downs),
        outs,
        mib=16,
        us=20 if own else 10,
    )


def add_kernel(ids, one_ref, two_ref, out_ref):
    out_ref[...] = one_ref[...].astype(F32) + two_ref[...].astype(F32)


def add(ids, one, two):
    return call(add_kernel, "add", ids, (one, two), shape(one.shape, F32), mib=8, us=20)


def mid_kernel(
    ids, own_grad, own_mixed, other_grad, other_got, other_mixed, cot_ref, gain_ref, o0, o1,
    grad_ref, own_ref, core_ref, low_own, low_other, part_ref,
):
    rows = own_grad.shape[0]
    other = other_grad[...].astype(F32) + other_got[...].astype(F32)
    for at, (grad_normed, mixed_ref) in enumerate(((own_grad[...], own_mixed), (other, other_mixed))):
        unit, factor = unit_rows(mixed_ref[...])
        scaled = grad_normed * gain_ref[...].astype(F32).reshape(1, -1)
        grad = factor * (scaled - unit * jnp.mean(scaled * unit, axis=-1, keepdims=True))
        grad = cot_ref[quarter_of(ids[2 * at], rows), :].astype(F32) + grad
        low = grad.astype(BF)
        (low_own, low_other)[at][...] = low
        if at == 0:
            grad_ref[...] = grad
            part_ref[...] = jnp.sum(grad_normed * unit, axis=0, keepdims=True)
        for o_ref, goal in ((o0, own_ref), (o1, core_ref)):
            goal[:, at * rows : (at + 1) * rows] = dot(o_ref[...], low, ((1,), (1,))).astype(BF)


def mid(ids, own, other, gain, cotangent, w_outputs):
    rows, width = own[0].shape
    columns = HEADS * HD
    outs = [
        shape((rows, width), F32), shape((columns, 2 * rows), BF), shape((columns, 2 * rows), BF), shape((rows, width), BF),
        shape((rows, width), BF), shape((1, width), F32),
    ]
    arrays = (*own, *other, cotangent, gain, *w_outputs)
    return call(mid_kernel, "mid", ids, arrays, outs, mib=16, us=0.01)


def back_kernel(*refs, first):
    ids, ea_ref, eb_ref, inv_a, inv_b, out_a, out_b, q_ref, k_ref, v_ref, grad_ref = refs[:11]
    refs = refs[11:]
    if first:
        ds_ref, dqa_ref, dqb_ref, key_ref, value_ref, near_ref, far_ref, x_ref = refs
    else:
        key_in, value_in, near_in, far_in, dqa_in, dqb_in = refs[:6]
        ds_ref, all_ref, near_ref, far_ref, x_ref = refs[6:]
    seq = k_ref.shape[0]
    width = seq // 4
    both = 2 * width
    lanes = width // 128
    base = 0 if first else 1
    sub = lax.broadcasted_iota(I32, (HD, both), 0)
    blocks = [ids[base + 2 * (l // lanes)] * lanes + l % lanes for l in range(2 * lanes)]
    mine = slice(base * width, (base + 1) * width)
    here = [quarter_of(ids[base + 2 * n], width) for n in range(2)]
    beside = lambda one, two: jnp.concatenate([one, two], axis=1)
    spot = lax.broadcasted_iota(I32, (8, 128), 0)

    def one_head(head, carry):
        cols = quarter_of(head, PAD)
        rows = pl.ds(pl.multiple_of(head * HD, HD), HD)
        grad = grad_ref[rows, :].astype(F32)
        grad = (grad * beside(inv_a[pl.ds(head, 1), mine], inv_b[pl.ds(head, 1), mine])).astype(BF).astype(F32)
        inner = jnp.sum(grad * beside(out_a[rows, mine], out_b[rows, mine]), axis=0, keepdims=True)
        high = inner.astype(BF).astype(F32)
        extra = jnp.where(sub == 0, -high, jnp.where(sub == 1, high - inner, 0.0))
        right = jnp.concatenate([grad, extra], axis=0).astype(BF)
        x_ref[...] = dot(v_ref[:, cols], right)
        value = dot(beside(ea_ref[head, :, mine], eb_ref[head, :, mine]), right, ((1,), (1,)))
        for c in range(seq // 16):
            at = slice(16 * c, 16 * c + 16)
            found = beside(ea_ref[head, at, mine], eb_ref[head, at, mine]).astype(F32)
            ds_ref[head, at, :] = (found * x_ref[at, :]).astype(BF)
        grad = ds_ref[head]
        key = dot(grad, jnp.concatenate([q_ref[at, cols] for at in here], axis=0))
        query = dot(k_ref[:, cols], grad, ((0,), (0,)))
        query_a = (query[:HD, :width] * 0.125).astype(BF)
        query_b = (query[:HD, width:] * 0.125).astype(BF)

        for g in range(NEAR // 2):
            total = None if first else near_in[head, 16 * g : 16 * g + 16]
            for l, block in enumerate(blocks):
                start = 128 * block - 96 + 16 * g
                inside = (start >= 0) & (start < seq)
                at = pl.ds(pl.multiple_of(jnp.clip(start, 0, seq - 16), 16), 16)
                found = ds_ref[head, at, 128 * l : 128 * l + 128].astype(F32)
                found = jnp.where(inside, found, 0.0)
                total = found if total is None else total + found
            near_ref[head, 16 * g : 16 * g + 16] = total
        for side in range(2):
            total = None if first else far_in[head, 8 * side : 8 * side + 8]
            for l, block in enumerate(blocks):
                marks = query[MARKS + 8 * side : MARKS + 8 * side + 8, 128 * l : 128 * l + 128]
                marks = jnp.where(spot == block, marks, 0.0)
                total = marks if total is None else total + marks
            far_ref[head, 8 * side : 8 * side + 8] = total

        if first:
            key_ref[:, cols] = key
            value_ref[:, cols] = value
            dqa_ref[rows, :] = query_a
            dqb_ref[rows, :] = query_b
        else:
            for k, found in enumerate((dqa_in[rows, :], query_a, dqb_in[rows, :], query_b)):
                all_ref[k, 0, rows, :] = found
            for part, acc in ((1, key_in[:, cols] + key), (2, value_in[:, cols] + value)):
                turned = acc.T[:HD].astype(BF)
                for q in range(4):
                    k = sum((jnp.where(ids[n] == q, n, 0) for n in range(1, 4)))
                    all_ref[k, part, rows, :] = turned[:, q * width : (q + 1) * width]
        return carry

    lax.fori_loop(0, HEADS, one_head, 0)


def back(ids, attended, queries, keys, values, grads, carried):
    seq, wide = queries.shape
    width = seq // 4
    first = carried is None
    columns = HEADS * HD
    queried = [shape((columns, width), BF)] * 2
    sums = [shape((seq, wide), F32)] * 2
    rel = [shape((HEADS, 8 * NEAR, 128), F32), shape((HEADS, 16, 128), F32)]
    outs = [shape((HEADS, seq, 2 * width), BF)]
    outs += queried + sums if first else [shape((4, 3, columns, width), BF)]
    outs += rel
    arrays = (*attended[0], *attended[1], *attended[2], queries, keys, values, grads, *(() if first else carried))
    return call(
        functools.partial(back_kernel, first=first),
        "back_first" if first else "back_last",
        ids,
        arrays,
        outs,
        mib=16,
        us=2 if first else 0.01,
        scratch=[pltpu.VMEM((seq, 2 * width), F32)],
    )


def places_kernel(ids, hor_ref, ver_ref, at_ref, both_ref):
    _, places, seq = at_ref.shape
    both_ref[0:1, :] = hor_ref[...]
    both_ref[1:2, :] = ver_ref[...]
    for axis, keys_ref in enumerate((hor_ref, ver_ref)):
        for b in range(places // 128):
            spot = lax.broadcasted_iota(I32, (128, seq), 0) + 128 * b
            at_ref[axis, 128 * b : 128 * b + 128, :] = jnp.where(spot == keys_ref[...], 1.0, 0.0).astype(BF)


def places_of(ids, hor, ver):
    seq = hor.shape[1]
    outs = [shape((2, PLACES, seq), BF), shape((2, seq), I32)]
    return call(places_kernel, "places", ids, (hor, ver), outs, mib=8, us=0.01)


def tables_kernel(ids, s_ref, e_ref, q_ref, *refs, base, axes):
    diagonals = refs[:-4]
    out_ref, left_ref, right_ref, found_ref = refs[-4:]
    width = s_ref.shape[2]
    groups = e_ref.shape[1] // 128

    def to_buckets(sums, delta):
        spot = lax.broadcasted_iota(I32, (32, sums.shape[1]), 0)
        return jnp.sum(jnp.where(bucket(delta) == spot, sums, 0.0), axis=1, keepdims=True)

    lane = lax.broadcasted_iota(I32, (1, 512), 1)
    spread = lax.broadcasted_iota(I32, (32, 128), 1)

    def heads_rows(column_of):
        add = lambda head, total: total + jnp.where(spread == head, column_of(head), 0.0)
        return lax.fori_loop(0, HEADS, add, jnp.zeros((32, 128), F32)).T[:8]

    def coordinate(axis, out_at):
        query = jnp.concatenate([q_ref[pl.ds(axis, 1), quarter_of(ids[base + n], width // 2)] for n in (0, 2)], axis=1)
        column = lax.broadcasted_iota(I32, (SPAN, width), 0)
        for b in range(groups):
            window = jnp.clip(128 * b + TOP - LOW - query, 0, TOP)
            right_ref[:, b * width : (b + 1) * width] = jnp.where(column == window, 1.0, 0.0).astype(BF)
        for head in range(HEADS):
            moved = dot(e_ref[axis], s_ref[head]).astype(BF)
            for b in range(groups):
                left_ref[head * 128 : head * 128 + 128, b * width : (b + 1) * width] = moved[128 * b : 128 * b + 128]
        found_ref[...] = dot(left_ref[...], right_ref[...], ((1,), (1,)))

        def column_of(head):
            grid = jnp.concatenate([found_ref[quarter_of(head, 128), :], jnp.zeros((128, 512 - SPAN), F32)], axis=1)
            grid = pltpu.roll(grid, 0, 1, stride=1, stride_axis=0)
            return to_buckets(jnp.sum(grid, axis=0, keepdims=True), lane + LOW - TOP)

        out_ref[out_at] = heads_rows(column_of)

    if len(axes) == 1:
        coordinate(axes[0], 0)
        return

    def one(axis, carry):
        coordinate(axis, axis)
        return carry

    lax.fori_loop(0, 2, one, 0)
    near_ref, far_ref = diagonals
    flip = 7 - lax.broadcasted_iota(I32, (8, 128), 0)
    spot = lax.broadcasted_iota(I32, (32, 1), 0)

    def near_column(head):
        near = [jnp.take_along_axis(near_ref[head, 8 * t : 8 * t + 8], flip, axis=0) for t in reversed(range(NEAR))]
        grid = jnp.concatenate(near, axis=0)
        grid = jnp.concatenate([grid, jnp.zeros((8 * NEAR, 384), F32)], axis=1)
        grid = pltpu.roll(grid, 0, 1, stride=1, stride_axis=0)
        near_sums = to_buckets(jnp.sum(grid, axis=0, keepdims=True), 8 * NEAR - 1 - 8 * 12 - lane)
        left = jnp.sum(jnp.sum(far_ref[head, :8], axis=0, keepdims=True), axis=1, keepdims=True)
        right = jnp.sum(jnp.sum(far_ref[head, 8:], axis=0, keepdims=True), axis=1, keepdims=True)
        return near_sums + jnp.where(spot == 15, left, 0.0) + jnp.where(spot == 31, right, 0.0)

    out_ref[2] = heads_rows(near_column)


def table_grads(ids, first, axes, scores, places, positions, sums=()):
    seq = positions.shape[1]
    wide = PLACES // 128 * seq // 2
    return call(
        functools.partial(tables_kernel, base=0 if first else 1, axes=axes),
        "table_grads",
        ids,
        (scores, places, positions, *sums),
        shape((3 if sums else 1, 8, 32), F32),
        mib=TABLES_MIB,
        us=0.01,
        scratch=[
            pltpu.VMEM((HEADS * 128, wide), BF), pltpu.VMEM((SPAN, wide), BF), pltpu.VMEM((HEADS * 128, SPAN), F32),
        ],
    )


def terms_of(grads, weights):
    total = None
    for part, w_ref in enumerate(weights):
        found = dot(grads[part], w_ref[...], ((0,), (0,)))
        total = found if total is None else total + found
    return total


def terms_send_kernel(ids, w0, w1, w2, grads_ref, *outs):
    for at, out_ref in enumerate(outs):
        out_ref[...] = terms_of(grads_ref[2 * at + 1], (w0, w1, w2)).astype(BF)


def terms_keep_kernel(ids, w0, w1, w2, grads_ref, got_own, got_other, own_ref, other_ref):
    other_ref[...] = (terms_of(grads_ref[2], (w0, w1, w2)) + got_other[...].astype(F32)).astype(BF)
    own_ref[...] = terms_of(grads_ref[0], (w0, w1, w2)) + got_own[...].astype(F32)


def terms_send(ids, weights, grads):
    outs = [shape((grads.shape[3], weights[0].shape[1]), BF)] * 2
    return call(terms_send_kernel, "terms_send", ids, (*weights, grads), outs, mib=16, us=0.01)


def terms_keep(ids, weights, grads, got):
    outs = [shape(got[0].shape, F32), shape(got[0].shape, BF)]
    return call(terms_keep_kernel, "terms_keep", ids, (*weights, grads, *got), outs, mib=16, us=0.01)


def last_kernel(
    ids, mine_ref, sent_ref, x_ref, page_ref, feat_ref, gain_ref, grad_ref, second_ref, mixed_ref, ffn_ref, got_ref,
    out_ref, part_ref,
):
    grad_normed = mine_ref[...] + sent_ref[...].astype(F32)
    here = quarter_of(ids[0], mine_ref.shape[0])
    unit, factor = unit_rows(hidden_rows(x_ref[here, :], page_ref[:, here], feat_ref[...]))
    scaled = grad_normed * gain_ref[...].astype(F32).reshape(1, -1)
    grad = factor * (scaled - unit * jnp.mean(scaled * unit, axis=-1, keepdims=True))
    rows, width = grad.shape
    out_ref[0, :rows] = (mixed_ref[...] + ffn_ref[...] + got_ref[...].astype(F32)).astype(BF)
    out_ref[1, :rows] = (grad_ref[...] + grad).astype(BF)
    part_ref[0:1] = jnp.sum(grad_normed * unit, axis=0, keepdims=True)
    part_ref[1:2] = second_ref[...]


def last(ids, mine, sent, inputs, onehot, feats, gain, grad_mixed, second, *ffn):
    rows, width = mine.shape
    arrays = (mine, sent, inputs, onehot, feats, gain, grad_mixed, second, *ffn)
    outs = [shape((2, rows, width), BF), shape((2, width), F32)]
    return call(last_kernel, "last", ids, arrays, outs, mib=16, us=0.01)


def pack_kernel(ids, gains_ref, got_ref, hor_a, ver_a, late, out_ref):
    gains = gains_ref[...] + got_ref[...]
    gains = [gains[slot : slot + 1] for slot in range(2)]
    parts = gains[0].shape[1] // 128
    for slot in range(2):
        gain = gains[slot]
        for part in range(parts):
            at = slot * parts + part
            out_ref[at : at + 1, :] = gain[:, part * 128 : part * 128 + 128]
    bins = hor_a.shape[2]
    at = 2 * parts
    out_ref[at:, :] = jnp.zeros((out_ref.shape[0] - at, 128), F32)
    for found in (late[2], hor_a[0] + late[0], ver_a[0] + late[1]):
        out_ref[at : at + HEADS, :bins] = found[:HEADS]
        at += HEADS


def pack(ids, gains, got, *sums):
    size = gains.shape[1] // 128 * 2 + 3 * HEADS
    size = -(-size // 8) * 8
    return call(pack_kernel, "pack", ids, (gains, got, *sums), shape((size, 128), F32), mib=8, us=0.1)


def join_kernel(ids, b0, b1, b2, b3, out_ref, *, slot):
    for k, b_ref in enumerate((b0, b1, b2, b3)):

        @pl.when(pl.program_id(0) == k)
        def _(b_ref=b_ref):
            out_ref[...] = b_ref[slot, : out_ref.shape[0]].astype(out_ref.dtype)


def join_feat_kernel(ids, b0, b1, b2, b3, page_ref, out_ref, feat_ref, all_ref, *, slot):
    step = pl.program_id(0)
    rows = out_ref.shape[0]
    for k, b_ref in enumerate((b0, b1, b2, b3)):

        @pl.when(step == k)
        def _(b_ref=b_ref, k=k):
            out_ref[...] = b_ref[slot, :rows].astype(out_ref.dtype)
            all_ref[pl.ds(pl.multiple_of(ids[k] * rows, rows), rows), :] = b_ref[slot, :rows]

    @pl.when(step == 3)
    def _():
        feat_ref[...] = dot(page_ref[...].astype(F32).astype(BF), all_ref[...])


def join(ids, blocks, slot, dtype, onehot=None):
    _, rows, width = blocks[0].shape
    specs = [VMEM] * 4
    outs, out_specs = [shape((4 * rows, width), dtype)], [pl.BlockSpec((rows, width), lambda i, s: (s[i], 0))]
    extra, scratch = (), []
    if onehot is not None:
        pages = onehot.shape[0]
        specs = specs + [VMEM]
        outs.append(shape((pages, width), F32))
        out_specs.append(whole((pages, width)))
        extra, scratch = (onehot,), [pltpu.VMEM((4 * rows, width), BF)]
    found = pl.pallas_call(
        functools.partial(join_kernel if onehot is None else join_feat_kernel, slot=slot),
        grid_spec=pltpu.PrefetchScalarGridSpec(
            num_scalar_prefetch=1, grid=(4,), in_specs=specs, out_specs=out_specs, scratch_shapes=scratch
        ),
        out_shape=outs,
        compiler_params=params(16),
        cost_estimate=cost(0.01),
        name="join_output" if onehot is None else "join_grads",
    )(ids, *blocks, *extra)
    return found[0] if onehot is None else found


def split_rows(ids, total, cols, keep_ref, send_ref, parity):
    groups, size = keep_ref.shape[0], keep_ref.shape[1]
    for g in range(groups):
        mine = pl.multiple_of((2 * g + parity) * size, 8)
        theirs = pl.multiple_of((2 * g + 1 - parity) * size, 8)
        keep_ref[g] = total[pl.ds(mine, size), cols].astype(keep_ref.dtype)
        send_ref[g] = total[pl.ds(theirs, size), cols].astype(BF)


def feed_grad_kernel(ids, k0, n0, k1, n1, c0, c1, cot_ref, *outs, fast):
    units = k0.shape[2]
    rows = lambda refs: jnp.concatenate(refs, axis=0)
    total = outs[-1]
    normed = rows([n0[2], c0[2], n1[2], c1[2]])
    total[:, :units] = dot(normed, rows([k0[1], c0[1], k1[1], c1[1]]), ((0,), (0,)))
    cotangent = rows([cot_ref[quarter_of(ids[n], k0.shape[1]), :] for n in range(4)])
    total[:, units:] = dot(cotangent, rows([k0[0], c0[0], k1[0], c1[0]]), ((0,), (0,)))
    if fast:
        split_rows(ids, total, slice(None), outs[0], outs[1], ids[9])
    else:
        outs[0][...] = total[...]


def feed_grad(ids, own, other, got_own, got_other, cotangent, fast):
    _, rows, units = own[0].shape
    width = cotangent.shape[1]
    if fast:
        outs = [shape((4, width // 8, 2 * units), F32), shape((4, width // 8, 2 * units), BF)]
    else:
        outs = [shape((width, 2 * units), F32)]
    return call(
        functools.partial(feed_grad_kernel, fast=fast),
        "feed_grad",
        ids,
        (*own, *other, got_own, got_other, cotangent),
        outs,
        mib=24,
        us=7,
        scratch=[pltpu.VMEM((width, 2 * units), F32)],
    )


def head_grad_kernel(ids, normed_ref, grads_ref, l0, l2, l1, l3, a0, a1, a2, a3, *outs, fast):
    total, turned = outs[-2:]
    n = a0.shape[0]
    normed = jnp.concatenate([normed_ref[quarter_of(ids[k], a0.shape[1]), :] for k in range(4)], axis=0)
    for part in range(3):
        left = jnp.concatenate([grads_ref[k, part] for k in range(4)], axis=1)
        total[part * n : (part + 1) * n, :] = dot(left, normed)
    low = jnp.concatenate([r[...] for r in (l0, l1, l2, l3)], axis=0)
    total[3 * n :, :] = dot(jnp.concatenate([r[...] for r in (a0, a1, a2, a3)], axis=1), low)
    turned[...] = total[...].T
    if fast:
        split_rows(ids, turned, slice(None), outs[0], outs[1], ids[9])
    else:
        outs[0][...] = turned[...]


def head_grad(ids, normed, grads, low, low_got, attended, fast):
    seq, width = normed.shape
    n = grads.shape[2]
    if fast:
        outs = [shape((4, width // 8, 4 * n), F32), shape((4, width // 8, 4 * n), BF)]
    else:
        outs = [shape((width, 4 * n), F32)]
    return call(
        functools.partial(head_grad_kernel, fast=fast),
        "head_grad",
        ids,
        (normed, grads, *low, *low_got, *attended),
        outs,
        mib=18,
        us=0.01,
        scratch=[pltpu.VMEM((4 * n, width), F32), pltpu.VMEM((width, 4 * n), F32)],
    )


def pair_kernel(ids, *refs):
    pairs, outs = refs[:-4], refs[-4:]
    for k, o_ref in enumerate(outs):
        at = ids[4 + k]
        start = 0
        for keep_ref, got_ref in zip(pairs[::2], pairs[1::2]):
            n = keep_ref.shape[2]
            o_ref[:, start : start + n] = (keep_ref[at] + got_ref[at].astype(F32)).astype(o_ref.dtype)
            start += n


def pair_sum(ids, *arrays):
    size = arrays[0].shape[1]
    n = sum(a.shape[2] for a in arrays[::2])
    outs = [shape((size, n), F32)] + [shape((size, n), BF)] * 3
    return call(pair_kernel, "pair_sum", ids, arrays, outs, mib=16, us=0.01)


def feed_final_kernel(a0, a1, a2, a3, up_ref, down_ref):
    total = a0[...] + a1[...].astype(F32) + a2[...].astype(F32) + a3[...].astype(F32)
    units = up_ref.shape[1]
    up_ref[...] = total[:, :units]
    down_ref[...] = total[:, units:]


def head_final_kernel(a0, a1, a2, a3, one_ref, two_ref, q_ref, k_ref, v_ref, o_ref, *smalls):
    total = a0[...] + a1[...].astype(F32) + a2[...].astype(F32) + a3[...].astype(F32)
    n = q_ref.shape[1]
    for at, goal in enumerate((q_ref, k_ref, v_ref)):
        goal[...] = total[:, at * n : (at + 1) * n]
    o_ref[...] = total[:, 3 * n :].T
    *tables, gains_ref = smalls
    total = one_ref[...] + two_ref[...]
    parts = gains_ref.shape[1] // 128
    for slot in range(2):
        for part in range(parts):
            at = slot * parts + part
            gains_ref[slot : slot + 1, part * 128 : part * 128 + 128] = total[at : at + 1]
    at, bins = 2 * parts, tables[0].shape[1]
    for goal in tables:
        goal[...] = total[at : at + HEADS, :bins]
        at += HEADS


def final(kernel, arrays, done, outs):
    arrays = [after(arrays[0], done)] + arrays[1:]
    return pl.pallas_call(
        kernel,
        grid=(1,),
        in_specs=[VMEM] * len(arrays),
        out_specs=jax.tree.map(lambda o: whole(o.shape), outs),
        out_shape=outs,
        compiler_params=params(16),
        cost_estimate=cost(5 if kernel is feed_final_kernel else 0.01),
        name=kernel.__name__[:-7],
    )(*arrays)


def swap(array, axis, size, bits):
    return lax.ppermute(array, axis, [(i, i ^ bits) for i in range(size)])


def after(array, *others):
    return lax.optimization_barrier((array, others))[0]


def local(
    inputs, page_feat, page_onehot, lengths, hor_pos, ver_pos, norm1_gain, w_query, w_key, w_value,
    rel_table, hor_table, ver_table, w_output, norm2_gain, w_up, w_down, cotangent, *, dp,
):
    seq, width = inputs.shape
    fast = dp == 8
    over = functools.partial(swap, axis="mp", size=4)
    m = lax.axis_index("mp").astype(I32)
    d = lax.axis_index("dp").astype(I32)
    k4 = jnp.arange(4, dtype=I32)
    spot = lambda who: (who & 1) * 2 + (who >> 1)
    ids = jnp.concatenate([
        spot(m ^ k4),
        (d >> 1) ^ k4,
        lengths[:1],
        (d & 1)[None],
    ])
    gain_one, gain_two = norm1_gain, norm2_gain
    feats = page_feat[0]
    hor, ver = hor_pos[None], ver_pos[None]
    tables = (rel_table, hor_table, ver_table)
    pages = page_onehot.T
    weights = [w_query.T, w_key.T, w_value.T]

    wo_y, wo_core = over(w_output, bits=2), over(w_output, bits=1)
    normed1, queries, keys, values = project(ids, inputs, pages, feats, gain_one, *weights)
    w_outputs = [w_output, wo_core, wo_y, over(after(wo_y, normed1), bits=1)]
    ups = [w_up, over(after(w_up, normed1), bits=1)]
    downs = [w_down, over(after(w_down, normed1), bits=1)]

    (e_a, att0, att1, inverse_a, out_a), lookups = attend(ids, queries, keys, values, hor, ver, tables, None)
    from_y, from_yc, own1 = over(att0, bits=2), over(att1, bits=3), over(att1, bits=1)
    ver_late = after(ver, att0, w_outputs[3], ups[1], downs[1])
    (e_b, att2, att3, inverse_b, out_b), _ = attend(ids, queries, keys, values, hor, ver_late, tables, lookups)
    attended = [att0, att1, att2, att3]
    for_other = [att2, over(att3, bits=1), from_y, from_yc]
    for_own = [att0, own1, over(att2, bits=2), over(att3, bits=3)]

    around = functools.partial(swap, axis="dp", size=dp)
    to_z = lambda parts: [parts[0]] + [around(part, bits=2 * k) for k, part in zip((1, 2, 3), parts[1:])]
    size = width // dp
    n = w_query.shape[1]
    units = w_up.shape[1]
    fixed = (inputs, pages, feats, gain_two, cotangent)
    x_keep, x_send, x_mixed, x_grad, x_ffn = feed(ids, False, *fixed, for_other, w_outputs, ups, downs)
    got_own, x_got = over(x_grad, bits=2), over(x_send, bits=1)
    for_own[0] = after(att0, x_ffn)
    m_keep, m_send, mixed, m_grad, m_ffn = feed(ids, True, *fixed, for_own, w_outputs, ups, downs)
    got_other, m_got = over(m_grad, bits=2), over(after(m_send, x_got), bits=1)
    own_grad = add(ids, m_grad, got_own)

    feed_grads = feed_grad(ids, (after(m_keep, own_grad), m_send), (x_keep, x_send), m_got, x_got, cotangent, fast)
    feed_got = around(feed_grads[1], bits=1) if fast else ids
    places_at, both = places_of(ids, after(hor, feed_grads[0]), ver)
    grad_mixed, ga, core_send, *low, gain_two_part = mid(
        ids, (after(own_grad, places_at), mixed), (x_grad, got_other, x_mixed), gain_two, cotangent, w_outputs[:2]
    )
    core_got = over(core_send, bits=1)
    sent_ffn = over(after(x_ffn, got_other, places_at), bits=2)

    halves = ((e_a, e_b), (inverse_a, inverse_b), (out_a, out_b))
    scores_a, dq0, dq2, key_sum, value_sum, near, far = back(ids, halves, queries, keys, values, ga, None)
    scores_b, grads, near, far = back(
        ids, halves, queries, keys, values, after(core_got, dq0), (key_sum, value_sum, near, far, dq0, dq2)
    )
    low_got = [over(part, bits=1) for part in low]
    to_core = terms_send(ids, weights, after(grads, sent_ffn))
    got_terms = [over(part, bits=1) for part in to_core]
    head_grads = head_grad(ids, normed1, after(grads, to_core[0]), low, low_got, attended, fast)
    own_terms, other_terms = terms_keep(ids, weights, after(grads, head_grads[0]), got_terms)
    sent_terms = over(other_terms, bits=2)

    hor_a = table_grads(ids, True, (0,), scores_a, places_at, after(both, own_terms))
    done = hor_a
    if fast:
        feed_parts = to_z(pair_sum(ids, after(feed_grads[0], done), feed_got))
        done = feed_parts[0]
    head_got = around(after(head_grads[1], done), bits=1) if fast else ids
    rows, gains = last(
        ids, after(own_terms, done), sent_terms, inputs, pages, feats, gain_one, grad_mixed, gain_two_part,
        mixed, m_ffn, sent_ffn,
    )
    rows_y, rows_core = over(rows, bits=2), over(rows, bits=1)
    ver_a = table_grads(ids, True, (1,), scores_a, places_at, after(both, rows))
    gains = after(gains, ver_a) + over(gains, bits=1)
    got_gains = over(gains, bits=2)
    late = table_grads(ids, False, (0, 1), scores_b, places_at, after(both, gains, head_got), (near, far))

    small = pack(ids, gains, got_gains, hor_a, ver_a, late)
    if fast:
        got = around(small, bits=1)
        grad_up, grad_down = final(feed_final_kernel, feed_parts, small, [shape((size, units), F32)] * 2)
        head_parts = to_z(pair_sum(ids, after(head_grads[0], grad_up), head_got))
        small = after(small, head_parts[0]) + got
        got = around(small, bits=2)
        quarters = [rows, rows_core, rows_y, over(after(rows_y, grad_up), bits=1)]
        outputs = join(ids, [after(rows, small)] + quarters[1:], 0, BF)
        grad_inputs, grad_feats = join(ids, [after(rows, outputs)] + quarters[1:], 1, F32, pages)
        small = after(small, grad_feats) + got
        bins = rel_table.shape[1]
        outs = [shape((size, n), F32)] * 3 + [shape((n, size), F32)] + [shape((HEADS, bins), F32)] * 3
        *found, gain_sums = final(
            head_final_kernel, head_parts + [small, around(small, bits=4)], grad_feats, outs + [shape((2, width), F32)]
        )
        grad_query, grad_key, grad_value, grad_output, grad_rel, grad_hor, grad_ver = found
    else:
        quarters = [rows, rows_core, rows_y, over(rows_y, bits=1)]
        outputs = join(ids, quarters, 0, BF)
        grad_inputs, grad_feats = join(ids, quarters, 1, F32, pages)
        small = lax.psum(small, "dp")
        scatter = lambda a: lax.psum_scatter(a[0], "dp", scatter_dimension=0, tiled=True)
        grad_feed, heads = scatter(feed_grads), scatter(head_grads)
        grad_up, grad_down = grad_feed[:, :units], grad_feed[:, units:]
        grad_query, grad_key, grad_value = heads[:, :n], heads[:, n : 2 * n], heads[:, 2 * n : 3 * n]
        grad_output = heads[:, 3 * n :].T
        gain_sums = small[: width // 128 * 2].reshape(2, width)
        table_sums = small[width // 128 * 2 :, : rel_table.shape[1]]
        grad_rel, grad_hor, grad_ver = (table_sums[at : at + HEADS] for at in range(0, 3 * HEADS, HEADS))
    gain_sums = lax.dynamic_slice(gain_sums, (0, d * size), (2, size))
    return (
        outputs, grad_inputs, grad_feats[None], gain_sums[0], grad_query, grad_key, grad_value,
        grad_rel, grad_hor, grad_ver, grad_output, gain_sums[1], grad_up, grad_down.T,
    )


def solution(mesh):
    return jax.shard_map(
        functools.partial(local, dp=mesh.shape["dp"]),
        mesh=mesh,
        in_specs=(
            P("dp", None),
            P("dp", None, None),
            P("dp", None),
            P("dp"),
            P("dp"),
            P("dp"),
            P(),
            P(None, "mp"),
            P(None, "mp"),
            P(None, "mp"),
            P("mp", None),
            P("mp", None),
            P("mp", None),
            P("mp", None),
            P(),
            P(None, "mp"),
            P("mp", None),
            P("dp", None),
        ),
        out_specs=(
            P("dp", None),
            P("dp", None),
            P("dp", None, None),
            P("dp"),
            P("dp", "mp"),
            P("dp", "mp"),
            P("dp", "mp"),
            P("mp", None),
            P("mp", None),
            P("mp", None),
            P("mp", "dp"),
            P("dp"),
            P("dp", "mp"),
            P("mp", "dp"),
        ),
        check_vma=False,
    )
```

profile of v0, /device:TPU:0, one launch (start us, length us, event | category | flops | bytes accessed | tf_op | source)
XLA Modules:
  0.0 144.8 jit_solution(6772976207985447973)
XLA Ops:
  0.6 3.0 %collective-permute-start = (bf16[192,768]{1,0:T(8,128)(2,1)}, bf16[192,768]{1,0:T(8,128)(2,1)S(1)}, u32[]{:S(2)}, u32[]{:S(2)}) collective-permute-start(bf16[192,768]{1,0:T(8,128)(2,1)} %o0.5), channel_id=1, source_target_pairs={{0,2},{1,3},{2,0},{3,1},{4,6},{5,7},{6,4},{7,5},{8,10},{9,11},{10,... | collective-permute-start | bytes 884744 | tf_op jit(solution)/shard_map/ppermute | solution.py:820
  4.4 1.4 copy-done.1
  10.9 4.2 %project.1 = (bf16[1024,768]{1,0:T(8,128)(2,1)S(1)}, bf16[1024,384]{1,0:T(8,128)(2,1)S(1)}, bf16[1024,384]{1,0:T(8,128)(2,1)S(1)}, bf16[1024,384]{1,0:T(8,128)(2,1)S(1)}) custom-call(s32[10]{0:T(128)S(1)} %pad_add_fusion.ids.refs_0_, bf16[1024,768]{1,0:T(8,128)(2,1)S(1)} %copy-done.1, s32[8,1024]{1,0:T(8,128)S(1)} %bitcast.23, bf16[8,768]{1,0:T(8,128)(2,1)S(1)} %bitcast.28, ...), custom_call_target="tpu_custom_call" | custom-call | flops 8049999872 | bytes 1 | tf_op jit(solution)/shard_map/project/pallas_call | solution.py:62
  16.3 10.2 %attend_first.1 = (bf16[3,1024,512]{2,1,0:T(8,128)(2,1)S(1)}, bf16[192,256]{1,0:T(8,128)(2,1)S(1)}, bf16[192,256]{1,0:T(8,128)(2,1)S(1)}, f32[3,512]{1,0:T(4,128...) custom-call(s32[10]{0:T(128)S(1)} %pad_add_fusion.ids.refs_0_, ...), custom_call_target="tpu_custom_call" | custom-call | flops 16099999744 | bytes 1 | tf_op jit(solution)/shard_map/attend_first/pallas_call | solution.py:62
  28.1 10.0 %attend_last.1 = (bf16[3,1024,512]{2,1,0:T(8,128)(2,1)S(1)}, bf16[192,256]{1,0:T(8,128)(2,1)S(1)}, bf16[192,256]{1,0:T(8,128)(2,1)S(1)}, f32[3,512]{1,0:T(4,128)S(1)}, f32[192,512]{1,0:T(8,128)S(1)}) custom-call(s32[10]{0:T(128)S(1)} %pad_add_fusion.ids.refs_0_, bf16[1024,384]{1,0:T(8,128)(2,1)S(1)} %get-tuple-element.120.refs_1_.refs_7_, ...), custom_call_target="tpu_custom_call" | custom-call | flops 16099999744 | bytes 1 | tf_op jit(solution)/shard_map/attend_last/pallas_call | solution.py:62
  39.1 1.9 %collective-permute-start.9 = (bf16[192,256]{1,0:T(8,128)(2,1)S(1)}, bf16[192,256]{1,0:T(8,128)(2,1)S(1)}, u32[]{:S(2)}, u32[]{:S(2)}) collective-permute-start(bf16[192,256]{1,0:T(8,128)(2,1)S(1)} %get-tuple-element.139.a0.a2), channel_id=1, source_target_pairs={{0,2},{1,3},{2,0},{3,1},{4,6},{5,7},{6,4},{7,5},{8,10},{9,11},{10,... | collective-permute-start | bytes 294920 | tf_op jit(solution)/shard_map/ppermute | solution.py:820
  41.1 4.6 %feed_other.1 = (bf16[2,256,768]{2,1,0:T(8,128)(2,1)S(1)}, bf16[3,256,768]{2,1,0:T(8,128)(2,1)S(1)}, f32[256,768]{1,0:T(8,128)S(1)}, bf16[256,768]{1,0:T(8,128)(2,1)S(1)}, bf16[256,768]{1,0:T(8,128)(2,1)S(1)}) custom-call(s32[10]{0:T(128)S(1)} %pad_add_fusion.ids.refs_0_, bf16[1024,768]{1,0:T(8,128)(2,1)S(1)} %copy-done.2, s32[8,1024]{1,0:T(8,128)S(1)} %bitcast.24, ...), custom_call_target="tpu_custom_call" | custom-call | flops 11500000256 | bytes 1 | tf_op jit(solution)/shard_map/feed_other/pallas_call | solution.py:62
  46.1 4.6 %feed_own.1 = (bf16[2,256,768]{2,1,0:T(8,128)(2,1)S(1)}, bf16[3,256,768]{2,1,0:T(8,128)(2,1)S(1)}, f32[256,768]{1,0:T(8,128)S(1)}, bf16[256,768]{1,0:T(8,128)(2,1)S(1)}, f32[256,768]{1,0:T(8,128)S(1)}) custom-call(s32[10]{0:T(128)S(1)} %pad_add_fusion.ids.refs_0_, bf16[1024,768]{1,0:T(8,128)(2,1)S(1)} %copy-done.2, s32[8,1024]{1,0:T(8,128)S(1)} %bitcast.25, ...), custom_call_target="tpu_custom_call" | custom-call | flops 23000000512 | bytes 1 | tf_op jit(solution)/shard_map/feed_own/pallas_call | solution.py:62
  50.7 1.8 %collective-permute-start.14 = (bf16[256,768]{1,0:T(8,128)(2,1)S(1)}, bf16[256,768]{1,0:T(8,128)(2,1)S(1)}, u32[]{:S(2)}, u32[]{:S(2)}) collective-permute-start(bf16[256,768]{1,0:T(8,128)(2,1)S(1)} %get-tuple-element.144.one_ref), channel_id=1, source_target_pairs={{0,2},{1,3},{2,0},{3,1},{4,6},{5,7},{6,4},{7,5},{8,10},{9,11},{10,... | collective-permute-start | bytes 1179656 | tf_op jit(solution)/shard_map/ppermute | solution.py:820
  52.5 5.2 %collective-permute-done.11.two_ref = bf16[256,768]{1,0:T(8,128)(2,1)S(1)} collective-permute-done((bf16[256,768]{1,0:T(8,128)(2,1)S(1)}, bf16[256,768]{1,0:T(8,128)(2,1)S(1)}, u32[]{:S(2)}, u32[]{:S(2)}) %collective-permute-start.11) | collective-permute-done | bytes 393248 | tf_op jit(solution)/shard_map/ppermute | solution.py:820
  58.4 3.4 %feed_grad.1 = (f32[4,96,1536]{2,1,0:T(8,128)S(1)}, bf16[4,96,1536]{2,1,0:T(8,128)(2,1)S(1)}) custom-call(s32[10]{0:T(128)S(1)} %pad_add_fusion.ids.refs_0_, bf16[2,256,768]{2,1,0:T(8,128)(2,1)S(1)} %get-tuple-element.147.k0, bf16[3,256,768]{2,1,0:T(8,128)(2,1)S(1)} %get-tuple-element.151.n0, bf16[2,256,768]{2,1,0:T(8,128)(2,1)S(1)} %get-tuple-element.149.k1, ...), custom_call_target="tpu_custom_call" | custom-call | flops 8049999872 | bytes 1 | tf_op jit(solution)/shard_map/feed_grad/pallas_call | solution.py:62
  61.8 1.6 %collective-permute-start.21 = (bf16[4,96,1536]{2,1,0:T(8,128)(2,1)S(1)}, bf16[4,96,1536]{2,1,0:T(8,128)(2,1)S(1)}, u32[]{:S(2)}, u32[]{:S(2)}) collective-permute-start(bf16[4,96,1536]{2,1,0:T(8,128)(2,1)S(1)} %get-tuple-element.182), channel_id=1, source_target_pairs={{0,4},{4,0},{8,12},{12,8},{16,20},{20,16},{24,28},{28,24},{1,5},{5... | collective-permute-start | bytes 3538952 | tf_op jit(solution)/shard_map/ppermute | solution.py:820
  66.0 1.8 %mid.1 = (f32[256,768]{1,0:T(8,128)S(1)}, bf16[192,512]{1,0:T(8,128)(2,1)S(1)}, bf16[192,512]{1,0:T(8,128)(2,1)S(1)}, bf16[256,768]{1,0:T(8,128)(2,1)S(1)}, bf16...) custom-call(s32[10]{0:T(128)S(1)} %pad_add_fusion.ids.refs_0_, f32[256,768]{1,0:T(8,128)S(1)} %add.28.own_grad, ...), custom_call_target="tpu_custom_call" | custom-call | flops 11500000 | bytes 1 | tf_op jit(solution)/shard_map/mid/pallas_call | solution.py:62
  68.4 4.7 %back_first.1 = (bf16[3,1024,512]{2,1,0:T(8,128)(2,1)S(1)}, bf16[192,256]{1,0:T(8,128)(2,1)S(1)}, bf16[192,256]{1,0:T(8,128)(2,1)S(1)}, f32[1024,384]{1,0:T(8,12...) custom-call(s32[10]{0:T(128)S(1)} %pad_add_fusion.ids.refs_0_, ...), custom_call_target="tpu_custom_call" | custom-call | flops 2300000000 | bytes 1 | tf_op jit(solution)/shard_map/back_first/pallas_call | solution.py:62
  73.2 4.6 %back_last.1 = (bf16[3,1024,512]{2,1,0:T(8,128)(2,1)S(1)}, bf16[4,3,192,256]{3,2,1,0:T(8,128)(2,1)S(1)}, f32[3,320,128]{2,1,0:T(8,128)S(1)}, f32[3,16,128]{2,1,0:T(8,128)S(1)}) custom-call(s32[10]{0:T(128)S(1)} %pad_add_fusion.ids.refs_0_, bf16[3,1024,512]{2,1,0:T(8,128)(2,1)S(1)} %get-tuple-element.123.refs_1_, ...), custom_call_target="tpu_custom_call" | custom-call | flops 11500000 | bytes 1 | tf_op jit(solution)/shard_map/back_last/pallas_call | solution.py:62
  79.9 2.2 %head_grad.1 = (f32[4,96,768]{2,1,0:T(8,128)S(1)}, bf16[4,96,768]{2,1,0:T(8,128)(2,1)S(1)}) custom-call(s32[10]{0:T(128)S(1)} %pad_add_fusion.ids.refs_0_, bf16[1024,768]{1,0:T(8,128)(2,1)S(1)} %get-tuple-element.125.normed_ref, bf16[4,3,192,256]{3,2,1,0:T(8,128)(2,1)S(1)} %get-tuple-element.175.grads_ref, bf16[256,768]{1,0:T(8,128)(2,1)S(1)} %get-tuple-element.172.l0, ...), custom_call_target="tpu_custom_call" | custom-call | flops 11500000 | bytes 1 | tf_op jit(solution)/shard_map/head_grad/pallas_call | solution.py:62
  83.5 1.8 %collective-permute-start.22 = (bf16[256,768]{1,0:T(8,128)(2,1)S(1)}, bf16[256,768]{1,0:T(8,128)(2,1)S(1)}, u32[]{:S(2)}, u32[]{:S(2)}) collective-permute-start(bf16[256,768]{1,0:T(8,128)(2,1)S(1)} %get-tuple-element.185), channel_id=1, source_target_pairs={{0,2},{1,3},{2,0},{3,1},{4,6},{5,7},{6,4},{7,5},{8,10},{9,11},{10,... | collective-permute-start | bytes 1179656 | tf_op jit(solution)/shard_map/ppermute | solution.py:820
  85.3 6.5 %table_grads.3.hor_a = f32[1,8,32]{2,1,0:T(8,128)S(1)} custom-call(s32[10]{0:T(128)S(1)} %pad_add_fusion.ids.refs_0_, bf16[3,1024,512]{2,1,0:T(8,128)(2,1)S(1)} %get-tuple-element.178.s_ref, bf16[2,1024,1024]{2,1,0:T(8,128)(2,1)S(1)} %get-tuple-element.154.e_ref, s32[2,1024]{1,0:T(2,128)S(1)} %get-tuple-element.196.q_ref), custom_call_target="tpu_custom_call" | custom-call | flops 11500000 | bytes 1 | tf_op jit(solution)/shard_map/table_grads/pallas_call | solution.py:62
  92.6 1.6 %collective-permute-start.25 = (bf16[4,96,768]{2,1,0:T(8,128)(2,1)S(1)}, bf16[4,96,768]{2,1,0:T(8,128)(2,1)S(1)}, u32[]{:S(2)}, u32[]{:S(2)}) collective-permute-start(bf16[4,96,768]{2,1,0:T(8,128)(2,1)S(1)} %get-tuple-element.195), channel_id=1, source_target_pairs={{0,4},{4,0},{8,12},{12,8},{16,20},{20,16},{24,28},{28,24},{1,5},{5... | collective-permute-start | bytes 1769480 | tf_op jit(solution)/shard_map/ppermute | solution.py:820
  94.1 1.6 %collective-permute-start.26 = (bf16[96,1536]{1,0:T(8,128)(2,1)S(1)}, bf16[96,1536]{1,0:T(8,128)(2,1)S(1)}, u32[]{:S(2)}, u32[]{:S(2)}) collective-permute-start(bf16[96,1536]{1,0:T(8,128)(2,1)S(1)} %get-tuple-element.200), channel_id=1, source_target_pairs={{0,8},{4,12},{8,0},{12,4},{16,24},{20,28},{24,16},{28,20},{1,9},{5... | collective-permute-start | bytes 884744 | tf_op jit(solution)/shard_map/ppermute | solution.py:820
  95.7 2.6 %collective-permute-start.27 = (bf16[96,1536]{1,0:T(8,128)(2,1)S(1)}, bf16[96,1536]{1,0:T(8,128)(2,1)S(1)}, u32[]{:S(2)}, u32[]{:S(2)}) collective-permute-start(bf16[96,1536]{1,0:T(8,128)(2,1)S(1)} %get-tuple-element.201), channel_id=1, source_target_pairs={{0,16},{4,20},{8,24},{12,28},{16,0},{20,4},{24,8},{28,12},{1,17},{... | collective-permute-start | bytes 884744 | tf_op jit(solution)/shard_map/ppermute | solution.py:820
  98.5 1.4 last.1
  101.7 6.3 %table_grads.4.ver_a = f32[1,8,32]{2,1,0:T(8,128)S(1)} custom-call(s32[10]{0:T(128)S(1)} %pad_add_fusion.ids.refs_0_, bf16[3,1024,512]{2,1,0:T(8,128)(2,1)S(1)} %get-tuple-element.178.s_ref, bf16[2,1024,1024]{2,1,0:T(8,128)(2,1)S(1)} %get-tuple-element.154.e_ref, s32[2,1024]{1,0:T(2,128)S(1)} %get-tuple-element.196.q_ref), custom_call_target="tpu_custom_call" | custom-call | flops 11500000 | bytes 1 | tf_op jit(solution)/shard_map/table_grads/pallas_call | solution.py:62
  108.0 1.6 %collective-permute-start.24 = (f32[2,768]{1,0:T(2,128)S(1)}, f32[2,768]{1,0:T(2,128)S(1)}, u32[]{:S(2)}, u32[]{:S(2)}) collective-permute-start(f32[2,768]{1,0:T(2,128)S(1)} %add.17.gains_ref), channel_id=1, source_target_pairs={{0,2},{1,3},{2,0},{3,1},{4,6},{5,7},{6,4},{7,5},{8,10},{9,11},{10,... | collective-permute-start | bytes 18440 | tf_op jit(solution)/shard_map/ppermute | solution.py:820
  109.6 12.8 %table_grads.5.late = f32[3,8,32]{2,1,0:T(8,128)S(1)} custom-call(s32[10]{0:T(128)S(1)} %pad_add_fusion.ids.refs_0_, bf16[3,1024,512]{2,1,0:T(8,128)(2,1)S(1)} %get-tuple-element.193.s_ref, bf16[2,1024,1024]{2,1,0:T(8,128)(2,1)S(1)} %get-tuple-element.154.e_ref, s32[2,1024]{1,0:T(2,128)S(1)} %get-tuple-element.196.q_ref, ...), custom_call_target="tpu_custom_call" | custom-call | flops 11500000 | bytes 1 | tf_op jit(solution)/shard_map/table_grads/pallas_call | solution.py:62
  125.6 1.6 %collective-permute-start.33 = (bf16[96,768]{1,0:T(8,128)(2,1)S(1)}, bf16[96,768]{1,0:T(8,128)(2,1)S(1)}, u32[]{:S(2)}, u32[]{:S(2)}) collective-permute-start(bf16[96,768]{1,0:T(8,128)(2,1)S(1)} %get-tuple-element.213), channel_id=1, source_target_pairs={{0,8},{4,12},{8,0},{12,4},{16,24},{20,28},{24,16},{28,20},{1,9},{5... | collective-permute-start | bytes 442376 | tf_op jit(solution)/shard_map/ppermute | solution.py:820
  127.1 2.7 %collective-permute-start.34 = (bf16[96,768]{1,0:T(8,128)(2,1)S(1)}, bf16[96,768]{1,0:T(8,128)(2,1)S(1)}, u32[]{:S(2)}, u32[]{:S(2)}) collective-permute-start(bf16[96,768]{1,0:T(8,128)(2,1)S(1)} %get-tuple-element.214), channel_id=1, source_target_pairs={{0,16},{4,20},{8,24},{12,28},{16,0},{20,4},{24,8},{28,12},{1,17},{... | collective-permute-start | bytes 442376 | tf_op jit(solution)/shard_map/ppermute | solution.py:820
  129.8 1.9 %collective-permute-start.35 = (bf16[96,768]{1,0:T(8,128)(2,1)S(1)}, bf16[96,768]{1,0:T(8,128)(2,1)S(1)}, u32[]{:S(2)}, u32[]{:S(2)}) collective-permute-start(bf16[96,768]{1,0:T(8,128)(2,1)S(1)} %get-tuple-element.215), channel_id=1, source_target_pairs={{0,24},{4,28},{8,16},{12,20},{16,8},{20,12},{24,0},{28,4},{1,25},{... | collective-permute-start | bytes 442376 | tf_op jit(solution)/shard_map/ppermute | solution.py:820
  131.7 2.3 %join_output.1 = bf16[1024,768]{1,0:T(8,128)(2,1)} custom-call(s32[10]{0:T(128)S(1)} %pad_add_fusion.ids.refs_0_, bf16[2,256,768]{2,1,0:T(8,128)(2,1)S(1)} %get-tuple-element.209.b0, bf16[2,256,768]{2,1,0:T(8,128)(2,1)S(1)} %collective-permute-done.30.b1, bf16[2,256,768]{2,1,0:T(8,128)(2,1)S(1)} %collective-permute-done.31.b2, ...), custom_call_target="tpu_custom_call" | custom-call | flops 11500000 | bytes 1 | tf_op jit(solution)/shard_map/join_output/pallas_call | solution.py:671
  134.0 3.1 %join_grads.1 = (f32[1024,768]{1,0:T(8,128)}, f32[8,768]{1,0:T(8,128)}) custom-call(s32[10]{0:T(128)S(1)} %pad_add_fusion.ids.refs_0_, bf16[2,256,768]{2,1,0:T(8,128)(2,1)S(1)} %get-tuple-element.209.b0, bf16[2,256,768]{2,1,0:T(8,128)(2,1)S(1)} %collective-permute-done.30.b1, bf16[2,256,768]{2,1,0:T(8,128)(2,1)S(1)} %collective-permute-done.31.b2, ...), custom_call_target="tpu_custom_call" | custom-call | flops 11500000 | bytes 1 | tf_op jit(solution)/shard_map/join_grads/pallas_call | solution.py:671
  137.0 3.4 %collective-permute-start.37 = (f32[24,128]{1,0:T(8,128)S(1)}, f32[24,128]{1,0:T(8,128)S(1)}, u32[]{:S(2)}, u32[]{:S(2)}) collective-permute-start(f32[24,128]{1,0:T(8,128)S(1)} %add.19.one_ref), channel_id=1, source_target_pairs={{0,16},{4,20},{8,24},{12,28},{16,0},{20,4},{24,8},{28,12},{1,17},{... | collective-permute-start | bytes 36872 | tf_op jit(solution)/shard_map/ppermute | solution.py:820
  141.1 2.2 %collective-permute-done.37.two_ref = f32[24,128]{1,0:T(8,128)S(1)} collective-permute-done((f32[24,128]{1,0:T(8,128)S(1)}, f32[24,128]{1,0:T(8,128)S(1)}, u32[]{:S(2)}, u32[]{:S(2)}) %collective-permute-start.37) | collective-permute-done | bytes 12320 | tf_op jit(solution)/shard_map/ppermute | solution.py:820
  (124 shorter events, 24.5 us)
Async XLA Ops:
  0.6 15.2 %collective-permute-start = (bf16[192,768]{1,0:T(8,128)(2,1)}, bf16[192,768]{1,0:T(8,128)(2,1)S(1)}, u32[]{:S(2)}, u32[]{:S(2)}) collective-permute-start(bf16[192,768]{1,0:T(8,128)(2,1)} %o0.5), channel_id=1, source_target_pairs={{0,2},{1,3},{2,0},{3,1},{4,6},{5,7},{6,4},{7,5},{8,10},{9,11},{10,... | collective-permute-start | bytes 884744 | tf_op jit(solution)/shard_map/ppermute | solution.py:820
  3.7 37.3 %collective-permute-start.7 = (bf16[192,768]{1,0:T(8,128)(2,1)}, bf16[192,768]{1,0:T(8,128)(2,1)S(1)}, u32[]{:S(2)}, u32[]{:S(2)}) collective-permute-start(bf16[192,768]{1,0:T(8,128)(2,1)} %o0.5), channel_id=1, source_target_pairs={{0,1},{1,0},{2,3},{3,2},{4,5},{5,4},{6,7},{7,6},{8,9},{9,8},{10,11... | collective-permute-start | bytes 884744 | tf_op jit(solution)/shard_map/ppermute | solution.py:820
  15.2 12.9 %collective-permute-start.2 = (bf16[768,768]{1,0:T(8,128)(2,1)S(1)}, bf16[768,768]{1,0:T(8,128)(2,1)S(1)}, u32[]{:S(2)}, u32[]{:S(2)}) collective-permute-start(bf16[768,768]{1,0:T(8,128)(2,1)S(1)} %copy-done.17), channel_id=1, source_target_pairs={{0,1},{1,0},{2,3},{3,2},{4,5},{5,4},{6,7},{7,6},{8,9},{9,8},{10,11... | collective-permute-start | bytes 3538952 | tf_op jit(solution)/shard_map/ppermute | solution.py:820
  15.8 12.3 %collective-permute-start.3 = (bf16[768,768]{1,0:T(8,128)(2,1)S(1)}, bf16[768,768]{1,0:T(8,128)(2,1)S(1)}, u32[]{:S(2)}, u32[]{:S(2)}) collective-permute-start(bf16[768,768]{1,0:T(8,128)(2,1)S(1)} %copy-done.18), channel_id=1, source_target_pairs={{0,1},{1,0},{2,3},{3,2},{4,5},{5,4},{6,7},{7,6},{8,9},{9,8},{10,11... | collective-permute-start | bytes 3538952 | tf_op jit(solution)/shard_map/ppermute | solution.py:820
  15.8 10.8 %collective-permute-start.1 = (bf16[192,768]{1,0:T(8,128)(2,1)S(1)}, bf16[192,768]{1,0:T(8,128)(2,1)S(1)}, u32[]{:S(2)}, u32[]{:S(2)}) collective-permute-start(bf16[192,768]{1,0:T(8,128)(2,1)S(1)} %collective-permute-done.o2), channel_id=1, source_target_pairs={{0,1},{1,0},{2,3},{3,2},{4,5},{5,4},{6,7},{7,6},{8,9},{9,8},{10,11... | collective-permute-start | bytes 884744 | tf_op jit(solution)/shard_map/ppermute | solution.py:820
  26.5 12.4 %collective-permute-start.5 = (bf16[192,256]{1,0:T(8,128)(2,1)S(1)}, bf16[192,256]{1,0:T(8,128)(2,1)S(1)}, u32[]{:S(2)}, u32[]{:S(2)}) collective-permute-start(bf16[192,256]{1,0:T(8,128)(2,1)S(1)} %get-tuple-element.143.a0), channel_id=1, source_target_pairs={{0,2},{1,3},{2,0},{3,1},{4,6},{5,7},{6,4},{7,5},{8,10},{9,11},{10,... | collective-permute-start | bytes 294920 | tf_op jit(solution)/shard_map/ppermute | solution.py:820
  26.7 12.4 %collective-permute-start.6 = (bf16[192,256]{1,0:T(8,128)(2,1)S(1)}, bf16[192,256]{1,0:T(8,128)(2,1)S(1)}, u32[]{:S(2)}, u32[]{:S(2)}) collective-permute-start(bf16[192,256]{1,0:T(8,128)(2,1)S(1)} %get-tuple-element.141.a1), channel_id=1, source_target_pairs={{0,3},{1,2},{2,1},{3,0},{4,7},{5,6},{6,5},{7,4},{8,11},{9,10},{10,... | collective-permute-start | bytes 294920 | tf_op jit(solution)/shard_map/ppermute | solution.py:820
  38.9 7.0 %collective-permute-start.8 = (bf16[192,256]{1,0:T(8,128)(2,1)S(1)}, bf16[192,256]{1,0:T(8,128)(2,1)S(1)}, u32[]{:S(2)}, u32[]{:S(2)}) collective-permute-start(bf16[192,256]{1,0:T(8,128)(2,1)S(1)} %get-tuple-element.141.a1), channel_id=1, source_target_pairs={{0,1},{1,0},{2,3},{3,2},{4,5},{5,4},{6,7},{7,6},{8,9},{9,8},{10,11... | collective-permute-start | bytes 294920 | tf_op jit(solution)/shard_map/ppermute | solution.py:820
  38.9 7.0 %collective-permute-start.10 = (bf16[192,256]{1,0:T(8,128)(2,1)S(1)}, bf16[192,256]{1,0:T(8,128)(2,1)S(1)}, u32[]{:S(2)}, u32[]{:S(2)}) collective-permute-start(bf16[192,256]{1,0:T(8,128)(2,1)S(1)} %get-tuple-element.140.a3), channel_id=1, source_target_pairs={{0,3},{1,2},{2,1},{3,0},{4,7},{5,6},{6,5},{7,4},{8,11},{9,10},{10,... | collective-permute-start | bytes 294920 | tf_op jit(solution)/shard_map/ppermute | solution.py:820
  39.1 7.1 %collective-permute-start.9 = (bf16[192,256]{1,0:T(8,128)(2,1)S(1)}, bf16[192,256]{1,0:T(8,128)(2,1)S(1)}, u32[]{:S(2)}, u32[]{:S(2)}) collective-permute-start(bf16[192,256]{1,0:T(8,128)(2,1)S(1)} %get-tuple-element.139.a0.a2), channel_id=1, source_target_pairs={{0,2},{1,3},{2,0},{3,1},{4,6},{5,7},{6,4},{7,5},{8,10},{9,11},{10,... | collective-permute-start | bytes 294920 | tf_op jit(solution)/shard_map/ppermute | solution.py:820
  45.7 6.8 %collective-permute-start.12 = (bf16[3,256,768]{2,1,0:T(8,128)(2,1)S(1)}, bf16[3,256,768]{2,1,0:T(8,128)(2,1)S(1)}, u32[]{:S(2)}, u32[]{:S(2)}) collective-permute-start(bf16[3,256,768]{2,1,0:T(8,128)(2,1)S(1)} %get-tuple-element.150.n1), channel_id=1, source_target_pairs={{0,1},{1,0},{2,3},{3,2},{4,5},{5,4},{6,7},{7,6},{8,9},{9,8},{10,11... | collective-permute-start | bytes 3538952 | tf_op jit(solution)/shard_map/ppermute | solution.py:820
  45.7 12.0 %collective-permute-start.11 = (bf16[256,768]{1,0:T(8,128)(2,1)S(1)}, bf16[256,768]{1,0:T(8,128)(2,1)S(1)}, u32[]{:S(2)}, u32[]{:S(2)}) collective-permute-start(bf16[256,768]{1,0:T(8,128)(2,1)S(1)} %get-tuple-element.145.other_grad), channel_id=1, source_target_pairs={{0,2},{1,3},{2,0},{3,1},{4,6},{5,7},{6,4},{7,5},{8,10},{9,11},{10,... | collective-permute-start | bytes 1179656 | tf_op jit(solution)/shard_map/ppermute | solution.py:820
  50.7 15.0 %collective-permute-start.14 = (bf16[256,768]{1,0:T(8,128)(2,1)S(1)}, bf16[256,768]{1,0:T(8,128)(2,1)S(1)}, u32[]{:S(2)}, u32[]{:S(2)}) collective-permute-start(bf16[256,768]{1,0:T(8,128)(2,1)S(1)} %get-tuple-element.144.one_ref), channel_id=1, source_target_pairs={{0,2},{1,3},{2,0},{3,1},{4,6},{5,7},{6,4},{7,5},{8,10},{9,11},{10,... | collective-permute-start | bytes 1179656 | tf_op jit(solution)/shard_map/ppermute | solution.py:820
  52.5 5.9 %collective-permute-start.13 = (bf16[3,256,768]{2,1,0:T(8,128)(2,1)S(1)}, bf16[3,256,768]{2,1,0:T(8,128)(2,1)S(1)}, u32[]{:S(2)}, u32[]{:S(2)}) collective-permute-start(bf16[3,256,768]{2,1,0:T(8,128)(2,1)S(1)} %get-tuple-element.151.n0), channel_id=1, source_target_pairs={{0,1},{1,0},{2,3},{3,2},{4,5},{5,4},{6,7},{7,6},{8,9},{9,8},{10,11... | collective-permute-start | bytes 3538952 | tf_op jit(solution)/shard_map/ppermute | solution.py:820
  61.8 30.0 %collective-permute-start.21 = (bf16[4,96,1536]{2,1,0:T(8,128)(2,1)S(1)}, bf16[4,96,1536]{2,1,0:T(8,128)(2,1)S(1)}, u32[]{:S(2)}, u32[]{:S(2)}) collective-permute-start(bf16[4,96,1536]{2,1,0:T(8,128)(2,1)S(1)} %get-tuple-element.182), channel_id=1, source_target_pairs={{0,4},{4,0},{8,12},{12,8},{16,20},{20,16},{24,28},{28,24},{1,5},{5... | collective-permute-start | bytes 3538952 | tf_op jit(solution)/shard_map/ppermute | solution.py:820
  65.7 12.2 %collective-permute-start.16 = (bf16[256,768]{1,0:T(8,128)(2,1)S(1)}, bf16[256,768]{1,0:T(8,128)(2,1)S(1)}, u32[]{:S(2)}, u32[]{:S(2)}) collective-permute-start(bf16[256,768]{1,0:T(8,128)(2,1)S(1)} %get-tuple-element.168), channel_id=1, source_target_pairs={{0,2},{1,3},{2,0},{3,1},{4,6},{5,7},{6,4},{7,5},{8,10},{9,11},{10,... | collective-permute-start | bytes 1179656 | tf_op jit(solution)/shard_map/ppermute | solution.py:820
  67.9 12.0 %collective-permute-start.17 = (bf16[256,768]{1,0:T(8,128)(2,1)S(1)}, bf16[256,768]{1,0:T(8,128)(2,1)S(1)}, u32[]{:S(2)}, u32[]{:S(2)}) collective-permute-start(bf16[256,768]{1,0:T(8,128)(2,1)S(1)} %get-tuple-element.172.l0), channel_id=1, source_target_pairs={{0,1},{1,0},{2,3},{3,2},{4,5},{5,4},{6,7},{7,6},{8,9},{9,8},{10,11... | collective-permute-start | bytes 1179656 | tf_op jit(solution)/shard_map/ppermute | solution.py:820
  68.4 11.5 %collective-permute-start.18 = (bf16[256,768]{1,0:T(8,128)(2,1)S(1)}, bf16[256,768]{1,0:T(8,128)(2,1)S(1)}, u32[]{:S(2)}, u32[]{:S(2)}) collective-permute-start(bf16[256,768]{1,0:T(8,128)(2,1)S(1)} %get-tuple-element.173.l2), channel_id=1, source_target_pairs={{0,1},{1,0},{2,3},{3,2},{4,5},{5,4},{6,7},{7,6},{8,9},{9,8},{10,11... | collective-permute-start | bytes 1179656 | tf_op jit(solution)/shard_map/ppermute | solution.py:820
  83.5 15.0 %collective-permute-start.22 = (bf16[256,768]{1,0:T(8,128)(2,1)S(1)}, bf16[256,768]{1,0:T(8,128)(2,1)S(1)}, u32[]{:S(2)}, u32[]{:S(2)}) collective-permute-start(bf16[256,768]{1,0:T(8,128)(2,1)S(1)} %get-tuple-element.185), channel_id=1, source_target_pairs={{0,2},{1,3},{2,0},{3,1},{4,6},{5,7},{6,4},{7,5},{8,10},{9,11},{10,... | collective-permute-start | bytes 1179656 | tf_op jit(solution)/shard_map/ppermute | solution.py:820
  92.6 15.5 %collective-permute-start.25 = (bf16[4,96,768]{2,1,0:T(8,128)(2,1)S(1)}, bf16[4,96,768]{2,1,0:T(8,128)(2,1)S(1)}, u32[]{:S(2)}, u32[]{:S(2)}) collective-permute-start(bf16[4,96,768]{2,1,0:T(8,128)(2,1)S(1)} %get-tuple-element.195), channel_id=1, source_target_pairs={{0,4},{4,0},{8,12},{12,8},{16,20},{20,16},{24,28},{28,24},{1,5},{5... | collective-permute-start | bytes 1769480 | tf_op jit(solution)/shard_map/ppermute | solution.py:820
  94.1 28.9 %collective-permute-start.26 = (bf16[96,1536]{1,0:T(8,128)(2,1)S(1)}, bf16[96,1536]{1,0:T(8,128)(2,1)S(1)}, u32[]{:S(2)}, u32[]{:S(2)}) collective-permute-start(bf16[96,1536]{1,0:T(8,128)(2,1)S(1)} %get-tuple-element.200), channel_id=1, source_target_pairs={{0,8},{4,12},{8,0},{12,4},{16,24},{20,28},{24,16},{28,20},{1,9},{5... | collective-permute-start | bytes 884744 | tf_op jit(solution)/shard_map/ppermute | solution.py:820
  95.7 27.3 %collective-permute-start.27 = (bf16[96,1536]{1,0:T(8,128)(2,1)S(1)}, bf16[96,1536]{1,0:T(8,128)(2,1)S(1)}, u32[]{:S(2)}, u32[]{:S(2)}) collective-permute-start(bf16[96,1536]{1,0:T(8,128)(2,1)S(1)} %get-tuple-element.201), channel_id=1, source_target_pairs={{0,16},{4,20},{8,24},{12,28},{16,0},{20,4},{24,8},{28,12},{1,17},{... | collective-permute-start | bytes 884744 | tf_op jit(solution)/shard_map/ppermute | solution.py:820
  98.3 24.7 %collective-permute-start.28 = (bf16[96,1536]{1,0:T(8,128)(2,1)S(1)}, bf16[96,1536]{1,0:T(8,128)(2,1)S(1)}, u32[]{:S(2)}, u32[]{:S(2)}) collective-permute-start(bf16[96,1536]{1,0:T(8,128)(2,1)S(1)} %get-tuple-element.202), channel_id=1, source_target_pairs={{0,24},{4,28},{8,16},{12,20},{16,8},{20,12},{24,0},{28,4},{1,25},{... | collective-permute-start | bytes 884744 | tf_op jit(solution)/shard_map/ppermute | solution.py:820
  101.2 22.7 %collective-permute-start.31 = (bf16[2,256,768]{2,1,0:T(8,128)(2,1)S(1)}, bf16[2,256,768]{2,1,0:T(8,128)(2,1)S(1)}, u32[]{:S(2)}, u32[]{:S(2)}) collective-permute-start(bf16[2,256,768]{2,1,0:T(8,128)(2,1)S(1)} %get-tuple-element.209.b0), channel_id=1, source_target_pairs={{0,2},{1,3},{2,0},{3,1},{4,6},{5,7},{6,4},{7,5},{8,10},{9,11},{10,... | collective-permute-start | bytes 2359304 | tf_op jit(solution)/shard_map/ppermute | solution.py:820
  108.0 14.3 %collective-permute-start.24 = (f32[2,768]{1,0:T(2,128)S(1)}, f32[2,768]{1,0:T(2,128)S(1)}, u32[]{:S(2)}, u32[]{:S(2)}) collective-permute-start(f32[2,768]{1,0:T(2,128)S(1)} %add.17.gains_ref), channel_id=1, source_target_pairs={{0,2},{1,3},{2,0},{3,1},{4,6},{5,7},{6,4},{7,5},{8,10},{9,11},{10,... | collective-permute-start | bytes 18440 | tf_op jit(solution)/shard_map/ppermute | solution.py:820
  122.4 9.3 %collective-permute-start.30 = (bf16[2,256,768]{2,1,0:T(8,128)(2,1)S(1)}, bf16[2,256,768]{2,1,0:T(8,128)(2,1)S(1)}, u32[]{:S(2)}, u32[]{:S(2)}) collective-permute-start(bf16[2,256,768]{2,1,0:T(8,128)(2,1)S(1)} %get-tuple-element.209.b0), channel_id=1, source_target_pairs={{0,1},{1,0},{2,3},{3,2},{4,5},{5,4},{6,7},{7,6},{8,9},{9,8},{10,11... | collective-permute-start | bytes 2359304 | tf_op jit(solution)/shard_map/ppermute | solution.py:820
  123.9 7.8 %collective-permute-start.32 = (bf16[2,256,768]{2,1,0:T(8,128)(2,1)S(1)}, bf16[2,256,768]{2,1,0:T(8,128)(2,1)S(1)}, u32[]{:S(2)}, u32[]{:S(2)}) collective-permute-start(bf16[2,256,768]{2,1,0:T(8,128)(2,1)S(1)} %collective-permute-done.31.b2), channel_id=1, source_target_pairs={{0,1},{1,0},{2,3},{3,2},{4,5},{5,4},{6,7},{7,6},{8,9},{9,8},{10,11... | collective-permute-start | bytes 2359304 | tf_op jit(solution)/shard_map/ppermute | solution.py:820
  124.4 5.4 %collective-permute-start.29 = (f32[24,128]{1,0:T(8,128)S(1)}, f32[24,128]{1,0:T(8,128)S(1)}, u32[]{:S(2)}, u32[]{:S(2)}) collective-permute-start(f32[24,128]{1,0:T(8,128)S(1)} %pack.1), channel_id=1, source_target_pairs={{0,4},{4,0},{8,12},{12,8},{16,20},{20,16},{24,28},{28,24},{1,5},{5... | collective-permute-start | bytes 36872 | tf_op jit(solution)/shard_map/ppermute | solution.py:820
  125.6 14.9 %collective-permute-start.33 = (bf16[96,768]{1,0:T(8,128)(2,1)S(1)}, bf16[96,768]{1,0:T(8,128)(2,1)S(1)}, u32[]{:S(2)}, u32[]{:S(2)}) collective-permute-start(bf16[96,768]{1,0:T(8,128)(2,1)S(1)} %get-tuple-element.213), channel_id=1, source_target_pairs={{0,8},{4,12},{8,0},{12,4},{16,24},{20,28},{24,16},{28,20},{1,9},{5... | collective-permute-start | bytes 442376 | tf_op jit(solution)/shard_map/ppermute | solution.py:820
  127.1 14.0 %collective-permute-start.34 = (bf16[96,768]{1,0:T(8,128)(2,1)S(1)}, bf16[96,768]{1,0:T(8,128)(2,1)S(1)}, u32[]{:S(2)}, u32[]{:S(2)}) collective-permute-start(bf16[96,768]{1,0:T(8,128)(2,1)S(1)} %get-tuple-element.214), channel_id=1, source_target_pairs={{0,16},{4,20},{8,24},{12,28},{16,0},{20,4},{24,8},{28,12},{1,17},{... | collective-permute-start | bytes 442376 | tf_op jit(solution)/shard_map/ppermute | solution.py:820
  129.8 11.3 %collective-permute-start.35 = (bf16[96,768]{1,0:T(8,128)(2,1)S(1)}, bf16[96,768]{1,0:T(8,128)(2,1)S(1)}, u32[]{:S(2)}, u32[]{:S(2)}) collective-permute-start(bf16[96,768]{1,0:T(8,128)(2,1)S(1)} %get-tuple-element.215), channel_id=1, source_target_pairs={{0,24},{4,28},{8,16},{12,20},{16,8},{20,12},{24,0},{28,4},{1,25},{... | collective-permute-start | bytes 442376 | tf_op jit(solution)/shard_map/ppermute | solution.py:820
  137.0 6.3 %collective-permute-start.37 = (f32[24,128]{1,0:T(8,128)S(1)}, f32[24,128]{1,0:T(8,128)S(1)}, u32[]{:S(2)}, u32[]{:S(2)}) collective-permute-start(f32[24,128]{1,0:T(8,128)S(1)} %add.19.one_ref), channel_id=1, source_target_pairs={{0,16},{4,20},{8,24},{12,28},{16,0},{20,4},{24,8},{28,12},{1,17},{... | collective-permute-start | bytes 36872 | tf_op jit(solution)/shard_map/ppermute | solution.py:820
  (30 other events, 161.5 us)
where the time goes:
time: 145 us
  Pallas kernels  91 us (63%)
  starting transfers between devices  34.1 us (24%)
  waiting for transfers between devices  10.7 us (7%)
  local copies, waits for them, and re-layouts  7.12 us (5%)
  between operations  1.78 us (1%)
    pallas_call x21, Pallas kernels, call(): pl.pallas_call(kernel, grid_spec=pltpu.PrefetchScalarGridSpec(num_scalar_...  84 us
    ppermute x38, starting transfers between devices, swap(): return lax.ppermute(array, axis, [(i, i ^ bits) for i in range(size)])  34.1 us
    ppermute x38, waiting for transfers between devices, swap(): return lax.ppermute(array, axis, [(i, i ^ bits) for i in range(size)])  10.7 us
    unnamed x48, local copies, waits for them, and re-layouts  6.53 us
    pallas_call x2, Pallas kernels, join(): pl.pallas_call(functools.partial(join_kernel if onehot is None else join_...  5.34 us
  transfers between devices with their start and end apart: 38, of which 6 were waited for; matrix products, arithmetic and copies ran while one was open for 0% of the time, Pallas kernels for 62%

commit v1 on v0

--- a/solution.py
+++ b/solution.py
@@ -89,7 +89,7 @@
 
 
 def project_kernel(ids, x_ref, page_ref, feat_ref, gain_ref, wq_ref, wk_ref, wv_ref, n_ref, q_ref, k_ref, v_ref):
-    rows = 256
+    rows = 512
 
     def block_of(step, carry):
         here = quarter_of(step, rows)
@@ -470,9 +470,13 @@
     both_ref[0:1, :] = hor_ref[...]
     both_ref[1:2, :] = ver_ref[...]
     for axis, keys_ref in enumerate((hor_ref, ver_ref)):
-        for b in range(places // 128):
+
+        def block(b, carry, axis=axis, keys_ref=keys_ref):
             spot = lax.broadcasted_iota(I32, (128, seq), 0) + 128 * b
-            at_ref[axis, 128 * b : 128 * b + 128, :] = jnp.where(spot == keys_ref[...], 1.0, 0.0).astype(BF)
+            at_ref[axis, quarter_of(b, 128), :] = jnp.where(spot == keys_ref[...], 1.0, 0.0).astype(BF)
+            return carry
+
+        lax.fori_loop(0, places // 128, block, 0)
 
 
 def places_of(ids, hor, ver):
@@ -495,8 +499,7 @@
     spread = lax.broadcasted_iota(I32, (32, 128), 1)
 
     def heads_rows(column_of):
-        add = lambda head, total: total + jnp.where(spread == head, column_of(head), 0.0)
-        return lax.fori_loop(0, HEADS, add, jnp.zeros((32, 128), F32)).T[:8]
+        return sum(jnp.where(spread == head, column_of(head), 0.0) for head in range(HEADS)).T[:8]
 
     def coordinate(axis, out_at):
         query = jnp.concatenate([q_ref[pl.ds(axis, 1), quarter_of(ids[base + n], width // 2)] for n in (0, 2)], axis=1)

time: 145 us -> 144 us (level)
  Pallas kernels: 91 us -> 88.1 us
    pallas_call x21, Pallas kernels: 84 us -> 81 us  [call(): pl.pallas_call(kernel, grid_spec=pltpu.PrefetchScalarGridSpec(num_scalar_...]
  transfers between devices with their start and end apart: 38 -> 38, of which waited for: 6 -> 8; matrix products, arithmetic and copies ran while one was open for 0% -> 0% of each run, Pallas kernels for 62% -> 61%
where the time goes in v1:
time: 144 us; the launch traced here: 143 us
  Pallas kernels  88.1 us (61%)
  starting transfers between devices  34.4 us (24%)
  waiting for transfers between devices  11.8 us (8%)
  local copies, waits for them, and re-layouts  7.12 us (5%)
  between operations  1.76 us (1%)
    pallas_call x21, Pallas kernels, call(): pl.pallas_call(kernel, grid_spec=pltpu.PrefetchScalarGridSpec(num_scalar_...  81 us
    ppermute x38, starting transfers between devices, swap(): return lax.ppermute(array, axis, [(i, i ^ bits) for i in range(size)])  34.4 us
    ppermute x38, waiting for transfers between devices, swap(): return lax.ppermute(array, axis, [(i, i ^ bits) for i in range(size)])  11.8 us
    unnamed x48, local copies, waits for them, and re-layouts  6.53 us
    pallas_call x2, Pallas kernels, join(): pl.pallas_call(functools.partial(join_kernel if onehot is None else join_...  5.33 us
  transfers between devices with their start and end apart: 38, of which 8 were waited for; matrix products, arithmetic and copies ran while one was open for 0% of the time, Pallas kernels for 61%

profile of v1, /device:TPU:0, one launch (start us, length us, event | category | flops | bytes accessed | tf_op | source)
XLA Modules:
  0.0 143.2 jit_solution(10915852645789022133)
XLA Ops:
  0.6 3.0 %collective-permute-start = (bf16[192,768]{1,0:T(8,128)(2,1)}, bf16[192,768]{1,0:T(8,128)(2,1)S(1)}, u32[]{:S(2)}, u32[]{:S(2)}) collective-permute-start(bf16[192,768]{1,0:T(8,128)(2,1)} %o0.5), channel_id=1, source_target_pairs={{0,2},{1,3},{2,0},{3,1},{4,6},{5,7},{6,4},{7,5},{8,10},{9,11},{10,... | collective-permute-start | bytes 884744 | tf_op jit(solution)/shard_map/ppermute | solution.py:823
  4.4 1.4 copy-done.1
  10.9 3.3 %project.1 = (bf16[1024,768]{1,0:T(8,128)(2,1)S(1)}, bf16[1024,384]{1,0:T(8,128)(2,1)S(1)}, bf16[1024,384]{1,0:T(8,128)(2,1)S(1)}, bf16[1024,384]{1,0:T(8,128)(2,1)S(1)}) custom-call(s32[10]{0:T(128)S(1)} %pad_add_fusion.ids.refs_0_, bf16[1024,768]{1,0:T(8,128)(2,1)S(1)} %copy-done.1, s32[8,1024]{1,0:T(8,128)S(1)} %bitcast.23, bf16[8,768]{1,0:T(8,128)(2,1)S(1)} %bitcast.28, ...), custom_call_target="tpu_custom_call" | custom-call | flops 8049999872 | bytes 1 | tf_op jit(solution)/shard_map/project/pallas_call | solution.py:62
  15.4 10.2 %attend_first.1 = (bf16[3,1024,512]{2,1,0:T(8,128)(2,1)S(1)}, bf16[192,256]{1,0:T(8,128)(2,1)S(1)}, bf16[192,256]{1,0:T(8,128)(2,1)S(1)}, f32[3,512]{1,0:T(4,128...) custom-call(s32[10]{0:T(128)S(1)} %pad_add_fusion.ids.refs_0_, ...), custom_call_target="tpu_custom_call" | custom-call | flops 16099999744 | bytes 1 | tf_op jit(solution)/shard_map/attend_first/pallas_call | solution.py:62
  25.7 1.4 collective-permute-start.6
  27.2 10.0 %attend_last.1 = (bf16[3,1024,512]{2,1,0:T(8,128)(2,1)S(1)}, bf16[192,256]{1,0:T(8,128)(2,1)S(1)}, bf16[192,256]{1,0:T(8,128)(2,1)S(1)}, f32[3,512]{1,0:T(4,128)S(1)}, f32[192,512]{1,0:T(8,128)S(1)}) custom-call(s32[10]{0:T(128)S(1)} %pad_add_fusion.ids.refs_0_, bf16[1024,384]{1,0:T(8,128)(2,1)S(1)} %get-tuple-element.120.refs_1_.refs_7_, ...), custom_call_target="tpu_custom_call" | custom-call | flops 16099999744 | bytes 1 | tf_op jit(solution)/shard_map/attend_last/pallas_call | solution.py:62
  38.2 1.9 %collective-permute-start.9 = (bf16[192,256]{1,0:T(8,128)(2,1)S(1)}, bf16[192,256]{1,0:T(8,128)(2,1)S(1)}, u32[]{:S(2)}, u32[]{:S(2)}) collective-permute-start(bf16[192,256]{1,0:T(8,128)(2,1)S(1)} %get-tuple-element.139.a0.a2), channel_id=1, source_target_pairs={{0,2},{1,3},{2,0},{3,1},{4,6},{5,7},{6,4},{7,5},{8,10},{9,11},{10,... | collective-permute-start | bytes 294920 | tf_op jit(solution)/shard_map/ppermute | solution.py:823
  40.2 4.6 %feed_other.1 = (bf16[2,256,768]{2,1,0:T(8,128)(2,1)S(1)}, bf16[3,256,768]{2,1,0:T(8,128)(2,1)S(1)}, f32[256,768]{1,0:T(8,128)S(1)}, bf16[256,768]{1,0:T(8,128)(2,1)S(1)}, bf16[256,768]{1,0:T(8,128)(2,1)S(1)}) custom-call(s32[10]{0:T(128)S(1)} %pad_add_fusion.ids.refs_0_, bf16[1024,768]{1,0:T(8,128)(2,1)S(1)} %copy-done.2, s32[8,1024]{1,0:T(8,128)S(1)} %bitcast.24, ...), custom_call_target="tpu_custom_call" | custom-call | flops 11500000256 | bytes 1 | tf_op jit(solution)/shard_map/feed_other/pallas_call | solution.py:62
  45.2 4.6 %feed_own.1 = (bf16[2,256,768]{2,1,0:T(8,128)(2,1)S(1)}, bf16[3,256,768]{2,1,0:T(8,128)(2,1)S(1)}, f32[256,768]{1,0:T(8,128)S(1)}, bf16[256,768]{1,0:T(8,128)(2,1)S(1)}, f32[256,768]{1,0:T(8,128)S(1)}) custom-call(s32[10]{0:T(128)S(1)} %pad_add_fusion.ids.refs_0_, bf16[1024,768]{1,0:T(8,128)(2,1)S(1)} %copy-done.2, s32[8,1024]{1,0:T(8,128)S(1)} %bitcast.25, ...), custom_call_target="tpu_custom_call" | custom-call | flops 23000000512 | bytes 1 | tf_op jit(solution)/shard_map/feed_own/pallas_call | solution.py:62
  49.8 1.8 %collective-permute-start.14 = (bf16[256,768]{1,0:T(8,128)(2,1)S(1)}, bf16[256,768]{1,0:T(8,128)(2,1)S(1)}, u32[]{:S(2)}, u32[]{:S(2)}) collective-permute-start(bf16[256,768]{1,0:T(8,128)(2,1)S(1)} %get-tuple-element.144.one_ref), channel_id=1, source_target_pairs={{0,2},{1,3},{2,0},{3,1},{4,6},{5,7},{6,4},{7,5},{8,10},{9,11},{10,... | collective-permute-start | bytes 1179656 | tf_op jit(solution)/shard_map/ppermute | solution.py:823
  51.6 5.2 %collective-permute-done.11.two_ref = bf16[256,768]{1,0:T(8,128)(2,1)S(1)} collective-permute-done((bf16[256,768]{1,0:T(8,128)(2,1)S(1)}, bf16[256,768]{1,0:T(8,128)(2,1)S(1)}, u32[]{:S(2)}, u32[]{:S(2)}) %collective-permute-start.11) | collective-permute-done | bytes 393248 | tf_op jit(solution)/shard_map/ppermute | solution.py:823
  57.5 3.4 %feed_grad.1 = (f32[4,96,1536]{2,1,0:T(8,128)S(1)}, bf16[4,96,1536]{2,1,0:T(8,128)(2,1)S(1)}) custom-call(s32[10]{0:T(128)S(1)} %pad_add_fusion.ids.refs_0_, bf16[2,256,768]{2,1,0:T(8,128)(2,1)S(1)} %get-tuple-element.147.k0, bf16[3,256,768]{2,1,0:T(8,128)(2,1)S(1)} %get-tuple-element.151.n0, bf16[2,256,768]{2,1,0:T(8,128)(2,1)S(1)} %get-tuple-element.149.k1, ...), custom_call_target="tpu_custom_call" | custom-call | flops 8049999872 | bytes 1 | tf_op jit(solution)/shard_map/feed_grad/pallas_call | solution.py:62
  60.9 1.6 %collective-permute-start.21 = (bf16[4,96,1536]{2,1,0:T(8,128)(2,1)S(1)}, bf16[4,96,1536]{2,1,0:T(8,128)(2,1)S(1)}, u32[]{:S(2)}, u32[]{:S(2)}) collective-permute-start(bf16[4,96,1536]{2,1,0:T(8,128)(2,1)S(1)} %get-tuple-element.182), channel_id=1, source_target_pairs={{0,4},{4,0},{8,12},{12,8},{16,20},{20,16},{24,28},{28,24},{1,5},{5... | collective-permute-start | bytes 3538952 | tf_op jit(solution)/shard_map/ppermute | solution.py:823
  65.1 1.8 %mid.1 = (f32[256,768]{1,0:T(8,128)S(1)}, bf16[192,512]{1,0:T(8,128)(2,1)S(1)}, bf16[192,512]{1,0:T(8,128)(2,1)S(1)}, bf16[256,768]{1,0:T(8,128)(2,1)S(1)}, bf16...) custom-call(s32[10]{0:T(128)S(1)} %pad_add_fusion.ids.refs_0_, f32[256,768]{1,0:T(8,128)S(1)} %add.28.own_grad, ...), custom_call_target="tpu_custom_call" | custom-call | flops 11500000 | bytes 1 | tf_op jit(solution)/shard_map/mid/pallas_call | solution.py:62
  67.5 4.5 %back_first.1 = (bf16[3,1024,512]{2,1,0:T(8,128)(2,1)S(1)}, bf16[192,256]{1,0:T(8,128)(2,1)S(1)}, bf16[192,256]{1,0:T(8,128)(2,1)S(1)}, f32[1024,384]{1,0:T(8,12...) custom-call(s32[10]{0:T(128)S(1)} %pad_add_fusion.ids.refs_0_, ...), custom_call_target="tpu_custom_call" | custom-call | flops 2300000000 | bytes 1 | tf_op jit(solution)/shard_map/back_first/pallas_call | solution.py:62
  72.1 4.9 %back_last.1 = (bf16[3,1024,512]{2,1,0:T(8,128)(2,1)S(1)}, bf16[4,3,192,256]{3,2,1,0:T(8,128)(2,1)S(1)}, f32[3,320,128]{2,1,0:T(8,128)S(1)}, f32[3,16,128]{2,1,0:T(8,128)S(1)}) custom-call(s32[10]{0:T(128)S(1)} %pad_add_fusion.ids.refs_0_, bf16[3,1024,512]{2,1,0:T(8,128)(2,1)S(1)} %get-tuple-element.123.refs_1_, ...), custom_call_target="tpu_custom_call" | custom-call | flops 11500000 | bytes 1 | tf_op jit(solution)/shard_map/back_last/pallas_call | solution.py:62
  79.0 2.2 %head_grad.1 = (f32[4,96,768]{2,1,0:T(8,128)S(1)}, bf16[4,96,768]{2,1,0:T(8,128)(2,1)S(1)}) custom-call(s32[10]{0:T(128)S(1)} %pad_add_fusion.ids.refs_0_, bf16[1024,768]{1,0:T(8,128)(2,1)S(1)} %get-tuple-element.125.normed_ref, bf16[4,3,192,256]{3,2,1,0:T(8,128)(2,1)S(1)} %get-tuple-element.175.grads_ref, bf16[256,768]{1,0:T(8,128)(2,1)S(1)} %get-tuple-element.172.l0, ...), custom_call_target="tpu_custom_call" | custom-call | flops 11500000 | bytes 1 | tf_op jit(solution)/shard_map/head_grad/pallas_call | solution.py:62
  82.6 1.8 %collective-permute-start.22 = (bf16[256,768]{1,0:T(8,128)(2,1)S(1)}, bf16[256,768]{1,0:T(8,128)(2,1)S(1)}, u32[]{:S(2)}, u32[]{:S(2)}) collective-permute-start(bf16[256,768]{1,0:T(8,128)(2,1)S(1)} %get-tuple-element.185), channel_id=1, source_target_pairs={{0,2},{1,3},{2,0},{3,1},{4,6},{5,7},{6,4},{7,5},{8,10},{9,11},{10,... | collective-permute-start | bytes 1179656 | tf_op jit(solution)/shard_map/ppermute | solution.py:823
  84.4 5.8 %table_grads.3.hor_a = f32[1,8,32]{2,1,0:T(8,128)S(1)} custom-call(s32[10]{0:T(128)S(1)} %pad_add_fusion.ids.refs_0_, bf16[3,1024,512]{2,1,0:T(8,128)(2,1)S(1)} %get-tuple-element.178.s_ref, bf16[2,1024,1024]{2,1,0:T(8,128)(2,1)S(1)} %get-tuple-element.154.e_ref, s32[2,1024]{1,0:T(2,128)S(1)} %get-tuple-element.196.q_ref), custom_call_target="tpu_custom_call" | custom-call | flops 11500000 | bytes 1 | tf_op jit(solution)/shard_map/table_grads/pallas_call | solution.py:62
  91.0 1.6 %collective-permute-start.25 = (bf16[4,96,768]{2,1,0:T(8,128)(2,1)S(1)}, bf16[4,96,768]{2,1,0:T(8,128)(2,1)S(1)}, u32[]{:S(2)}, u32[]{:S(2)}) collective-permute-start(bf16[4,96,768]{2,1,0:T(8,128)(2,1)S(1)} %get-tuple-element.195), channel_id=1, source_target_pairs={{0,4},{4,0},{8,12},{12,8},{16,20},{20,16},{24,28},{28,24},{1,5},{5... | collective-permute-start | bytes 1769480 | tf_op jit(solution)/shard_map/ppermute | solution.py:823
  92.6 1.6 %collective-permute-start.26 = (bf16[96,1536]{1,0:T(8,128)(2,1)S(1)}, bf16[96,1536]{1,0:T(8,128)(2,1)S(1)}, u32[]{:S(2)}, u32[]{:S(2)}) collective-permute-start(bf16[96,1536]{1,0:T(8,128)(2,1)S(1)} %get-tuple-element.200), channel_id=1, source_target_pairs={{0,8},{4,12},{8,0},{12,4},{16,24},{20,28},{24,16},{28,20},{1,9},{5... | collective-permute-start | bytes 884744 | tf_op jit(solution)/shard_map/ppermute | solution.py:823
  94.2 2.6 %collective-permute-start.27 = (bf16[96,1536]{1,0:T(8,128)(2,1)S(1)}, bf16[96,1536]{1,0:T(8,128)(2,1)S(1)}, u32[]{:S(2)}, u32[]{:S(2)}) collective-permute-start(bf16[96,1536]{1,0:T(8,128)(2,1)S(1)} %get-tuple-element.201), channel_id=1, source_target_pairs={{0,16},{4,20},{8,24},{12,28},{16,0},{20,4},{24,8},{28,12},{1,17},{... | collective-permute-start | bytes 884744 | tf_op jit(solution)/shard_map/ppermute | solution.py:823
  97.0 1.4 last.1
  100.2 5.8 %table_grads.4.ver_a = f32[1,8,32]{2,1,0:T(8,128)S(1)} custom-call(s32[10]{0:T(128)S(1)} %pad_add_fusion.ids.refs_0_, bf16[3,1024,512]{2,1,0:T(8,128)(2,1)S(1)} %get-tuple-element.178.s_ref, bf16[2,1024,1024]{2,1,0:T(8,128)(2,1)S(1)} %get-tuple-element.154.e_ref, s32[2,1024]{1,0:T(2,128)S(1)} %get-tuple-element.196.q_ref), custom_call_target="tpu_custom_call" | custom-call | flops 11500000 | bytes 1 | tf_op jit(solution)/shard_map/table_grads/pallas_call | solution.py:62
  107.6 11.8 %table_grads.5.late = f32[3,8,32]{2,1,0:T(8,128)S(1)} custom-call(s32[10]{0:T(128)S(1)} %pad_add_fusion.ids.refs_0_, bf16[3,1024,512]{2,1,0:T(8,128)(2,1)S(1)} %get-tuple-element.193.s_ref, bf16[2,1024,1024]{2,1,0:T(8,128)(2,1)S(1)} %get-tuple-element.154.e_ref, s32[2,1024]{1,0:T(2,128)S(1)} %get-tuple-element.196.q_ref, ...), custom_call_target="tpu_custom_call" | custom-call | flops 11500000 | bytes 1 | tf_op jit(solution)/shard_map/table_grads/pallas_call | solution.py:62
  122.9 2.4 %collective-permute-start.33 = (bf16[96,768]{1,0:T(8,128)(2,1)S(1)}, bf16[96,768]{1,0:T(8,128)(2,1)S(1)}, u32[]{:S(2)}, u32[]{:S(2)}) collective-permute-start(bf16[96,768]{1,0:T(8,128)(2,1)S(1)} %get-tuple-element.213), channel_id=1, source_target_pairs={{0,8},{4,12},{8,0},{12,4},{16,24},{20,28},{24,16},{28,20},{1,9},{5... | collective-permute-start | bytes 442376 | tf_op jit(solution)/shard_map/ppermute | solution.py:823
  125.3 1.9 %collective-permute-start.34 = (bf16[96,768]{1,0:T(8,128)(2,1)S(1)}, bf16[96,768]{1,0:T(8,128)(2,1)S(1)}, u32[]{:S(2)}, u32[]{:S(2)}) collective-permute-start(bf16[96,768]{1,0:T(8,128)(2,1)S(1)} %get-tuple-element.214), channel_id=1, source_target_pairs={{0,16},{4,20},{8,24},{12,28},{16,0},{20,4},{24,8},{28,12},{1,17},{... | collective-permute-start | bytes 442376 | tf_op jit(solution)/shard_map/ppermute | solution.py:823
  127.2 1.5 %collective-permute-start.35 = (bf16[96,768]{1,0:T(8,128)(2,1)S(1)}, bf16[96,768]{1,0:T(8,128)(2,1)S(1)}, u32[]{:S(2)}, u32[]{:S(2)}) collective-permute-start(bf16[96,768]{1,0:T(8,128)(2,1)S(1)} %get-tuple-element.215), channel_id=1, source_target_pairs={{0,24},{4,28},{8,16},{12,20},{16,8},{20,12},{24,0},{28,4},{1,25},{... | collective-permute-start | bytes 442376 | tf_op jit(solution)/shard_map/ppermute | solution.py:823
  129.3 2.3 %join_output.1 = bf16[1024,768]{1,0:T(8,128)(2,1)} custom-call(s32[10]{0:T(128)S(1)} %pad_add_fusion.ids.refs_0_, bf16[2,256,768]{2,1,0:T(8,128)(2,1)S(1)} %get-tuple-element.209.b0, bf16[2,256,768]{2,1,0:T(8,128)(2,1)S(1)} %collective-permute-done.30.b1, bf16[2,256,768]{2,1,0:T(8,128)(2,1)S(1)} %collective-permute-done.31.b2, ...), custom_call_target="tpu_custom_call" | custom-call | flops 11500000 | bytes 1 | tf_op jit(solution)/shard_map/join_output/pallas_call | solution.py:674
  131.6 3.1 %join_grads.1 = (f32[1024,768]{1,0:T(8,128)}, f32[8,768]{1,0:T(8,128)}) custom-call(s32[10]{0:T(128)S(1)} %pad_add_fusion.ids.refs_0_, bf16[2,256,768]{2,1,0:T(8,128)(2,1)S(1)} %get-tuple-element.209.b0, bf16[2,256,768]{2,1,0:T(8,128)(2,1)S(1)} %collective-permute-done.30.b1, bf16[2,256,768]{2,1,0:T(8,128)(2,1)S(1)} %collective-permute-done.31.b2, ...), custom_call_target="tpu_custom_call" | custom-call | flops 11500000 | bytes 1 | tf_op jit(solution)/shard_map/join_grads/pallas_call | solution.py:674
  135.4 3.5 %collective-permute-start.37 = (f32[24,128]{1,0:T(8,128)S(1)}, f32[24,128]{1,0:T(8,128)S(1)}, u32[]{:S(2)}, u32[]{:S(2)}) collective-permute-start(f32[24,128]{1,0:T(8,128)S(1)} %add.19.one_ref), channel_id=1, source_target_pairs={{0,16},{4,20},{8,24},{12,28},{16,0},{20,4},{24,8},{28,12},{1,17},{... | collective-permute-start | bytes 36872 | tf_op jit(solution)/shard_map/ppermute | solution.py:823
  139.2 2.6 %collective-permute-done.37.two_ref = f32[24,128]{1,0:T(8,128)S(1)} collective-permute-done((f32[24,128]{1,0:T(8,128)S(1)}, f32[24,128]{1,0:T(8,128)S(1)}, u32[]{:S(2)}, u32[]{:S(2)}) %collective-permute-start.37) | collective-permute-done | bytes 12320 | tf_op jit(solution)/shard_map/ppermute | solution.py:823
  (124 shorter events, 26.1 us)
Async XLA Ops:
  0.6 14.3 %collective-permute-start = (bf16[192,768]{1,0:T(8,128)(2,1)}, bf16[192,768]{1,0:T(8,128)(2,1)S(1)}, u32[]{:S(2)}, u32[]{:S(2)}) collective-permute-start(bf16[192,768]{1,0:T(8,128)(2,1)} %o0.5), channel_id=1, source_target_pairs={{0,2},{1,3},{2,0},{3,1},{4,6},{5,7},{6,4},{7,5},{8,10},{9,11},{10,... | collective-permute-start | bytes 884744 | tf_op jit(solution)/shard_map/ppermute | solution.py:823
  3.7 36.4 %collective-permute-start.7 = (bf16[192,768]{1,0:T(8,128)(2,1)}, bf16[192,768]{1,0:T(8,128)(2,1)S(1)}, u32[]{:S(2)}, u32[]{:S(2)}) collective-permute-start(bf16[192,768]{1,0:T(8,128)(2,1)} %o0.5), channel_id=1, source_target_pairs={{0,1},{1,0},{2,3},{3,2},{4,5},{5,4},{6,7},{7,6},{8,9},{9,8},{10,11... | collective-permute-start | bytes 884744 | tf_op jit(solution)/shard_map/ppermute | solution.py:823
  14.3 12.9 %collective-permute-start.2 = (bf16[768,768]{1,0:T(8,128)(2,1)S(1)}, bf16[768,768]{1,0:T(8,128)(2,1)S(1)}, u32[]{:S(2)}, u32[]{:S(2)}) collective-permute-start(bf16[768,768]{1,0:T(8,128)(2,1)S(1)} %copy-done.17), channel_id=1, source_target_pairs={{0,1},{1,0},{2,3},{3,2},{4,5},{5,4},{6,7},{7,6},{8,9},{9,8},{10,11... | collective-permute-start | bytes 3538952 | tf_op jit(solution)/shard_map/ppermute | solution.py:823
  14.8 12.3 %collective-permute-start.3 = (bf16[768,768]{1,0:T(8,128)(2,1)S(1)}, bf16[768,768]{1,0:T(8,128)(2,1)S(1)}, u32[]{:S(2)}, u32[]{:S(2)}) collective-permute-start(bf16[768,768]{1,0:T(8,128)(2,1)S(1)} %copy-done.18), channel_id=1, source_target_pairs={{0,1},{1,0},{2,3},{3,2},{4,5},{5,4},{6,7},{7,6},{8,9},{9,8},{10,11... | collective-permute-start | bytes 3538952 | tf_op jit(solution)/shard_map/ppermute | solution.py:823
  14.9 10.8 %collective-permute-start.1 = (bf16[192,768]{1,0:T(8,128)(2,1)S(1)}, bf16[192,768]{1,0:T(8,128)(2,1)S(1)}, u32[]{:S(2)}, u32[]{:S(2)}) collective-permute-start(bf16[192,768]{1,0:T(8,128)(2,1)S(1)} %collective-permute-done.o2), channel_id=1, source_target_pairs={{0,1},{1,0},{2,3},{3,2},{4,5},{5,4},{6,7},{7,6},{8,9},{9,8},{10,11... | collective-permute-start | bytes 884744 | tf_op jit(solution)/shard_map/ppermute | solution.py:823
  25.6 12.4 %collective-permute-start.5 = (bf16[192,256]{1,0:T(8,128)(2,1)S(1)}, bf16[192,256]{1,0:T(8,128)(2,1)S(1)}, u32[]{:S(2)}, u32[]{:S(2)}) collective-permute-start(bf16[192,256]{1,0:T(8,128)(2,1)S(1)} %get-tuple-element.143.a0), channel_id=1, source_target_pairs={{0,2},{1,3},{2,0},{3,1},{4,6},{5,7},{6,4},{7,5},{8,10},{9,11},{10,... | collective-permute-start | bytes 294920 | tf_op jit(solution)/shard_map/ppermute | solution.py:823
  25.7 12.4 %collective-permute-start.6 = (bf16[192,256]{1,0:T(8,128)(2,1)S(1)}, bf16[192,256]{1,0:T(8,128)(2,1)S(1)}, u32[]{:S(2)}, u32[]{:S(2)}) collective-permute-start(bf16[192,256]{1,0:T(8,128)(2,1)S(1)} %get-tuple-element.141.a1), channel_id=1, source_target_pairs={{0,3},{1,2},{2,1},{3,0},{4,7},{5,6},{6,5},{7,4},{8,11},{9,10},{10,... | collective-permute-start | bytes 294920 | tf_op jit(solution)/shard_map/ppermute | solution.py:823
  38.0 7.1 %collective-permute-start.8 = (bf16[192,256]{1,0:T(8,128)(2,1)S(1)}, bf16[192,256]{1,0:T(8,128)(2,1)S(1)}, u32[]{:S(2)}, u32[]{:S(2)}) collective-permute-start(bf16[192,256]{1,0:T(8,128)(2,1)S(1)} %get-tuple-element.141.a1), channel_id=1, source_target_pairs={{0,1},{1,0},{2,3},{3,2},{4,5},{5,4},{6,7},{7,6},{8,9},{9,8},{10,11... | collective-permute-start | bytes 294920 | tf_op jit(solution)/shard_map/ppermute | solution.py:823
  38.0 7.0 %collective-permute-start.10 = (bf16[192,256]{1,0:T(8,128)(2,1)S(1)}, bf16[192,256]{1,0:T(8,128)(2,1)S(1)}, u32[]{:S(2)}, u32[]{:S(2)}) collective-permute-start(bf16[192,256]{1,0:T(8,128)(2,1)S(1)} %get-tuple-element.140.a3), channel_id=1, source_target_pairs={{0,3},{1,2},{2,1},{3,0},{4,7},{5,6},{6,5},{7,4},{8,11},{9,10},{10,... | collective-permute-start | bytes 294920 | tf_op jit(solution)/shard_map/ppermute | solution.py:823
  38.2 7.1 %collective-permute-start.9 = (bf16[192,256]{1,0:T(8,128)(2,1)S(1)}, bf16[192,256]{1,0:T(8,128)(2,1)S(1)}, u32[]{:S(2)}, u32[]{:S(2)}) collective-permute-start(bf16[192,256]{1,0:T(8,128)(2,1)S(1)} %get-tuple-element.139.a0.a2), channel_id=1, source_target_pairs={{0,2},{1,3},{2,0},{3,1},{4,6},{5,7},{6,4},{7,5},{8,10},{9,11},{10,... | collective-permute-start | bytes 294920 | tf_op jit(solution)/shard_map/ppermute | solution.py:823
  44.8 6.8 %collective-permute-start.12 = (bf16[3,256,768]{2,1,0:T(8,128)(2,1)S(1)}, bf16[3,256,768]{2,1,0:T(8,128)(2,1)S(1)}, u32[]{:S(2)}, u32[]{:S(2)}) collective-permute-start(bf16[3,256,768]{2,1,0:T(8,128)(2,1)S(1)} %get-tuple-element.150.n1), channel_id=1, source_target_pairs={{0,1},{1,0},{2,3},{3,2},{4,5},{5,4},{6,7},{7,6},{8,9},{9,8},{10,11... | collective-permute-start | bytes 3538952 | tf_op jit(solution)/shard_map/ppermute | solution.py:823
  44.8 12.0 %collective-permute-start.11 = (bf16[256,768]{1,0:T(8,128)(2,1)S(1)}, bf16[256,768]{1,0:T(8,128)(2,1)S(1)}, u32[]{:S(2)}, u32[]{:S(2)}) collective-permute-start(bf16[256,768]{1,0:T(8,128)(2,1)S(1)} %get-tuple-element.145.other_grad), channel_id=1, source_target_pairs={{0,2},{1,3},{2,0},{3,1},{4,6},{5,7},{6,4},{7,5},{8,10},{9,11},{10,... | collective-permute-start | bytes 1179656 | tf_op jit(solution)/shard_map/ppermute | solution.py:823
  49.8 15.0 %collective-permute-start.14 = (bf16[256,768]{1,0:T(8,128)(2,1)S(1)}, bf16[256,768]{1,0:T(8,128)(2,1)S(1)}, u32[]{:S(2)}, u32[]{:S(2)}) collective-permute-start(bf16[256,768]{1,0:T(8,128)(2,1)S(1)} %get-tuple-element.144.one_ref), channel_id=1, source_target_pairs={{0,2},{1,3},{2,0},{3,1},{4,6},{5,7},{6,4},{7,5},{8,10},{9,11},{10,... | collective-permute-start | bytes 1179656 | tf_op jit(solution)/shard_map/ppermute | solution.py:823
  51.6 5.9 %collective-permute-start.13 = (bf16[3,256,768]{2,1,0:T(8,128)(2,1)S(1)}, bf16[3,256,768]{2,1,0:T(8,128)(2,1)S(1)}, u32[]{:S(2)}, u32[]{:S(2)}) collective-permute-start(bf16[3,256,768]{2,1,0:T(8,128)(2,1)S(1)} %get-tuple-element.151.n0), channel_id=1, source_target_pairs={{0,1},{1,0},{2,3},{3,2},{4,5},{5,4},{6,7},{7,6},{8,9},{9,8},{10,11... | collective-permute-start | bytes 3538952 | tf_op jit(solution)/shard_map/ppermute | solution.py:823
  60.9 29.4 %collective-permute-start.21 = (bf16[4,96,1536]{2,1,0:T(8,128)(2,1)S(1)}, bf16[4,96,1536]{2,1,0:T(8,128)(2,1)S(1)}, u32[]{:S(2)}, u32[]{:S(2)}) collective-permute-start(bf16[4,96,1536]{2,1,0:T(8,128)(2,1)S(1)} %get-tuple-element.182), channel_id=1, source_target_pairs={{0,4},{4,0},{8,12},{12,8},{16,20},{20,16},{24,28},{28,24},{1,5},{5... | collective-permute-start | bytes 3538952 | tf_op jit(solution)/shard_map/ppermute | solution.py:823
  64.8 12.2 %collective-permute-start.16 = (bf16[256,768]{1,0:T(8,128)(2,1)S(1)}, bf16[256,768]{1,0:T(8,128)(2,1)S(1)}, u32[]{:S(2)}, u32[]{:S(2)}) collective-permute-start(bf16[256,768]{1,0:T(8,128)(2,1)S(1)} %get-tuple-element.168), channel_id=1, source_target_pairs={{0,2},{1,3},{2,0},{3,1},{4,6},{5,7},{6,4},{7,5},{8,10},{9,11},{10,... | collective-permute-start | bytes 1179656 | tf_op jit(solution)/shard_map/ppermute | solution.py:823
  66.9 12.0 %collective-permute-start.17 = (bf16[256,768]{1,0:T(8,128)(2,1)S(1)}, bf16[256,768]{1,0:T(8,128)(2,1)S(1)}, u32[]{:S(2)}, u32[]{:S(2)}) collective-permute-start(bf16[256,768]{1,0:T(8,128)(2,1)S(1)} %get-tuple-element.172.l0), channel_id=1, source_target_pairs={{0,1},{1,0},{2,3},{3,2},{4,5},{5,4},{6,7},{7,6},{8,9},{9,8},{10,11... | collective-permute-start | bytes 1179656 | tf_op jit(solution)/shard_map/ppermute | solution.py:823
  67.4 11.5 %collective-permute-start.18 = (bf16[256,768]{1,0:T(8,128)(2,1)S(1)}, bf16[256,768]{1,0:T(8,128)(2,1)S(1)}, u32[]{:S(2)}, u32[]{:S(2)}) collective-permute-start(bf16[256,768]{1,0:T(8,128)(2,1)S(1)} %get-tuple-element.173.l2), channel_id=1, source_target_pairs={{0,1},{1,0},{2,3},{3,2},{4,5},{5,4},{6,7},{7,6},{8,9},{9,8},{10,11... | collective-permute-start | bytes 1179656 | tf_op jit(solution)/shard_map/ppermute | solution.py:823
  82.6 14.4 %collective-permute-start.22 = (bf16[256,768]{1,0:T(8,128)(2,1)S(1)}, bf16[256,768]{1,0:T(8,128)(2,1)S(1)}, u32[]{:S(2)}, u32[]{:S(2)}) collective-permute-start(bf16[256,768]{1,0:T(8,128)(2,1)S(1)} %get-tuple-element.185), channel_id=1, source_target_pairs={{0,2},{1,3},{2,0},{3,1},{4,6},{5,7},{6,4},{7,5},{8,10},{9,11},{10,... | collective-permute-start | bytes 1179656 | tf_op jit(solution)/shard_map/ppermute | solution.py:823
  91.0 15.5 %collective-permute-start.25 = (bf16[4,96,768]{2,1,0:T(8,128)(2,1)S(1)}, bf16[4,96,768]{2,1,0:T(8,128)(2,1)S(1)}, u32[]{:S(2)}, u32[]{:S(2)}) collective-permute-start(bf16[4,96,768]{2,1,0:T(8,128)(2,1)S(1)} %get-tuple-element.195), channel_id=1, source_target_pairs={{0,4},{4,0},{8,12},{12,8},{16,20},{20,16},{24,28},{28,24},{1,5},{5... | collective-permute-start | bytes 1769480 | tf_op jit(solution)/shard_map/ppermute | solution.py:823
  92.6 27.4 %collective-permute-start.26 = (bf16[96,1536]{1,0:T(8,128)(2,1)S(1)}, bf16[96,1536]{1,0:T(8,128)(2,1)S(1)}, u32[]{:S(2)}, u32[]{:S(2)}) collective-permute-start(bf16[96,1536]{1,0:T(8,128)(2,1)S(1)} %get-tuple-element.200), channel_id=1, source_target_pairs={{0,8},{4,12},{8,0},{12,4},{16,24},{20,28},{24,16},{28,20},{1,9},{5... | collective-permute-start | bytes 884744 | tf_op jit(solution)/shard_map/ppermute | solution.py:823
  94.2 25.8 %collective-permute-start.27 = (bf16[96,1536]{1,0:T(8,128)(2,1)S(1)}, bf16[96,1536]{1,0:T(8,128)(2,1)S(1)}, u32[]{:S(2)}, u32[]{:S(2)}) collective-permute-start(bf16[96,1536]{1,0:T(8,128)(2,1)S(1)} %get-tuple-element.201), channel_id=1, source_target_pairs={{0,16},{4,20},{8,24},{12,28},{16,0},{20,4},{24,8},{28,12},{1,17},{... | collective-permute-start | bytes 884744 | tf_op jit(solution)/shard_map/ppermute | solution.py:823
  96.7 23.3 %collective-permute-start.28 = (bf16[96,1536]{1,0:T(8,128)(2,1)S(1)}, bf16[96,1536]{1,0:T(8,128)(2,1)S(1)}, u32[]{:S(2)}, u32[]{:S(2)}) collective-permute-start(bf16[96,1536]{1,0:T(8,128)(2,1)S(1)} %get-tuple-element.202), channel_id=1, source_target_pairs={{0,24},{4,28},{8,16},{12,20},{16,8},{20,12},{24,0},{28,4},{1,25},{... | collective-permute-start | bytes 884744 | tf_op jit(solution)/shard_map/ppermute | solution.py:823
  99.6 21.2 %collective-permute-start.31 = (bf16[2,256,768]{2,1,0:T(8,128)(2,1)S(1)}, bf16[2,256,768]{2,1,0:T(8,128)(2,1)S(1)}, u32[]{:S(2)}, u32[]{:S(2)}) collective-permute-start(bf16[2,256,768]{2,1,0:T(8,128)(2,1)S(1)} %get-tuple-element.209.b0), channel_id=1, source_target_pairs={{0,2},{1,3},{2,0},{3,1},{4,6},{5,7},{6,4},{7,5},{8,10},{9,11},{10,... | collective-permute-start | bytes 2359304 | tf_op jit(solution)/shard_map/ppermute | solution.py:823
  106.5 12.9 %collective-permute-start.24 = (f32[2,768]{1,0:T(2,128)S(1)}, f32[2,768]{1,0:T(2,128)S(1)}, u32[]{:S(2)}, u32[]{:S(2)}) collective-permute-start(f32[2,768]{1,0:T(2,128)S(1)} %add.17.gains_ref), channel_id=1, source_target_pairs={{0,2},{1,3},{2,0},{3,1},{4,6},{5,7},{6,4},{7,5},{8,10},{9,11},{10,... | collective-permute-start | bytes 18440 | tf_op jit(solution)/shard_map/ppermute | solution.py:823
  119.4 9.3 %collective-permute-start.30 = (bf16[2,256,768]{2,1,0:T(8,128)(2,1)S(1)}, bf16[2,256,768]{2,1,0:T(8,128)(2,1)S(1)}, u32[]{:S(2)}, u32[]{:S(2)}) collective-permute-start(bf16[2,256,768]{2,1,0:T(8,128)(2,1)S(1)} %get-tuple-element.209.b0), channel_id=1, source_target_pairs={{0,1},{1,0},{2,3},{3,2},{4,5},{5,4},{6,7},{7,6},{8,9},{9,8},{10,11... | collective-permute-start | bytes 2359304 | tf_op jit(solution)/shard_map/ppermute | solution.py:823
  120.9 8.4 %collective-permute-start.32 = (bf16[2,256,768]{2,1,0:T(8,128)(2,1)S(1)}, bf16[2,256,768]{2,1,0:T(8,128)(2,1)S(1)}, u32[]{:S(2)}, u32[]{:S(2)}) collective-permute-start(bf16[2,256,768]{2,1,0:T(8,128)(2,1)S(1)} %collective-permute-done.31.b2), channel_id=1, source_target_pairs={{0,1},{1,0},{2,3},{3,2},{4,5},{5,4},{6,7},{7,6},{8,9},{9,8},{10,11... | collective-permute-start | bytes 2359304 | tf_op jit(solution)/shard_map/ppermute | solution.py:823
  122.9 16.0 %collective-permute-start.33 = (bf16[96,768]{1,0:T(8,128)(2,1)S(1)}, bf16[96,768]{1,0:T(8,128)(2,1)S(1)}, u32[]{:S(2)}, u32[]{:S(2)}) collective-permute-start(bf16[96,768]{1,0:T(8,128)(2,1)S(1)} %get-tuple-element.213), channel_id=1, source_target_pairs={{0,8},{4,12},{8,0},{12,4},{16,24},{20,28},{24,16},{28,20},{1,9},{5... | collective-permute-start | bytes 442376 | tf_op jit(solution)/shard_map/ppermute | solution.py:823
  125.3 13.9 %collective-permute-start.34 = (bf16[96,768]{1,0:T(8,128)(2,1)S(1)}, bf16[96,768]{1,0:T(8,128)(2,1)S(1)}, u32[]{:S(2)}, u32[]{:S(2)}) collective-permute-start(bf16[96,768]{1,0:T(8,128)(2,1)S(1)} %get-tuple-element.214), channel_id=1, source_target_pairs={{0,16},{4,20},{8,24},{12,28},{16,0},{20,4},{24,8},{28,12},{1,17},{... | collective-permute-start | bytes 442376 | tf_op jit(solution)/shard_map/ppermute | solution.py:823
  127.2 12.1 %collective-permute-start.35 = (bf16[96,768]{1,0:T(8,128)(2,1)S(1)}, bf16[96,768]{1,0:T(8,128)(2,1)S(1)}, u32[]{:S(2)}, u32[]{:S(2)}) collective-permute-start(bf16[96,768]{1,0:T(8,128)(2,1)S(1)} %get-tuple-element.215), channel_id=1, source_target_pairs={{0,24},{4,28},{8,16},{12,20},{16,8},{20,12},{24,0},{28,4},{1,25},{... | collective-permute-start | bytes 442376 | tf_op jit(solution)/shard_map/ppermute | solution.py:823
  128.7 6.7 %collective-permute-start.36 = (f32[24,128]{1,0:T(8,128)S(1)}, f32[24,128]{1,0:T(8,128)S(1)}, u32[]{:S(2)}, u32[]{:S(2)}) collective-permute-start(f32[24,128]{1,0:T(8,128)S(1)} %add.18), channel_id=1, source_target_pairs={{0,8},{4,12},{8,0},{12,4},{16,24},{20,28},{24,16},{28,20},{1,9},{5... | collective-permute-start | bytes 36872 | tf_op jit(solution)/shard_map/ppermute | solution.py:823
  135.4 6.4 %collective-permute-start.37 = (f32[24,128]{1,0:T(8,128)S(1)}, f32[24,128]{1,0:T(8,128)S(1)}, u32[]{:S(2)}, u32[]{:S(2)}) collective-permute-start(f32[24,128]{1,0:T(8,128)S(1)} %add.19.one_ref), channel_id=1, source_target_pairs={{0,16},{4,20},{8,24},{12,28},{16,0},{20,4},{24,8},{28,12},{1,17},{... | collective-permute-start | bytes 36872 | tf_op jit(solution)/shard_map/ppermute | solution.py:823
  (30 other events, 156.0 us)

commit v2 on v1

--- a/solution.py
+++ b/solution.py
@@ -786,37 +786,39 @@
     down_ref[...] = total[:, units:]
 
 
-def head_final_kernel(a0, a1, a2, a3, one_ref, two_ref, q_ref, k_ref, v_ref, o_ref, *smalls):
+def head_final_kernel(ids, a0, a1, a2, a3, one_ref, two_ref, q_ref, k_ref, v_ref, o_ref, *smalls):
     total = a0[...] + a1[...].astype(F32) + a2[...].astype(F32) + a3[...].astype(F32)
     n = q_ref.shape[1]
     for at, goal in enumerate((q_ref, k_ref, v_ref)):
         goal[...] = total[:, at * n : (at + 1) * n]
     o_ref[...] = total[:, 3 * n :].T
-    *tables, gains_ref = smalls
+    *tables, gain_one, gain_two = smalls
     total = one_ref[...] + two_ref[...]
-    parts = gains_ref.shape[1] // 128
-    for slot in range(2):
-        for part in range(parts):
-            at = slot * parts + part
-            gains_ref[slot : slot + 1, part * 128 : part * 128 + 128] = total[at : at + 1]
+    size = gain_one.shape[1]
+    width = 8 * size
+    parts = width // 128
+    mine = lax.rem(width - (2 * ids[4] + ids[9]) * size, width)
+    for slot, goal in enumerate((gain_one, gain_two)):
+        gain = jnp.concatenate([total[slot * parts + part : slot * parts + part + 1] for part in range(parts)], axis=1)
+        goal[...] = pltpu.roll(jnp.broadcast_to(gain, (8, width)), mine, 1)[:1, :size]
     at, bins = 2 * parts, tables[0].shape[1]
     for goal in tables:
         goal[...] = total[at : at + HEADS, :bins]
         at += HEADS
 
 
-def final(kernel, arrays, done, outs):
+def final(kernel, arrays, done, outs, *ids):
     arrays = [after(arrays[0], done)] + arrays[1:]
     return pl.pallas_call(
         kernel,
         grid=(1,),
-        in_specs=[VMEM] * len(arrays),
+        in_specs=[pl.BlockSpec(memory_space=pltpu.SMEM)] * len(ids) + [VMEM] * len(arrays),
         out_specs=jax.tree.map(lambda o: whole(o.shape), outs),
         out_shape=outs,
         compiler_params=params(16),
         cost_estimate=cost(5 if kernel is feed_final_kernel else 0.01),
         name=kernel.__name__[:-7],
-    )(*arrays)
+    )(*ids, *arrays)
 
 
 def swap(array, axis, size, bits):
@@ -928,8 +930,8 @@
         small = after(small, grad_feats) + got
         bins = rel_table.shape[1]
         outs = [shape((size, n), F32)] * 3 + [shape((n, size), F32)] + [shape((HEADS, bins), F32)] * 3
-        *found, gain_sums = final(
-            head_final_kernel, head_parts + [small, around(small, bits=4)], grad_feats, outs + [shape((2, width), F32)]
+        *found, first_gain, second_gain = final(
+            head_final_kernel, head_parts + [small, around(small, bits=4)], grad_feats, outs + [shape((1, size), F32)] * 2, ids
         )
         grad_query, grad_key, grad_value, grad_output, grad_rel, grad_hor, grad_ver = found
     else:
@@ -942,13 +944,13 @@
         grad_up, grad_down = grad_feed[:, :units], grad_feed[:, units:]
         grad_query, grad_key, grad_value = heads[:, :n], heads[:, n : 2 * n], heads[:, 2 * n : 3 * n]
         grad_output = heads[:, 3 * n :].T
-        gain_sums = small[: width // 128 * 2].reshape(2, width)
+        gain_sums = lax.dynamic_slice(small[: width // 128 * 2].reshape(2, width), (0, d * size), (2, size))
+        first_gain, second_gain = gain_sums[:1], gain_sums[1:]
         table_sums = small[width // 128 * 2 :, : rel_table.shape[1]]
         grad_rel, grad_hor, grad_ver = (table_sums[at : at + HEADS] for at in range(0, 3 * HEADS, HEADS))
-    gain_sums = lax.dynamic_slice(gain_sums, (0, d * size), (2, size))
     return (
-        outputs, grad_inputs, grad_feats[None], gain_sums[0], grad_query, grad_key, grad_value,
-        grad_rel, grad_hor, grad_ver, grad_output, gain_sums[1], grad_up, grad_down.T,
+        outputs, grad_inputs, grad_feats[None], first_gain[0], grad_query, grad_key, grad_value,
+        grad_rel, grad_hor, grad_ver, grad_output, second_gain[0], grad_up, grad_down.T,
     )
 
 

time: 144 us -> 144 us (level)
  no operation moved by 1% of the time
where the time goes in v2:
time: 144 us; the launch traced here: 143 us
  Pallas kernels  88.6 us (62%)
  starting transfers between devices  34.4 us (24%)
  waiting for transfers between devices  11.8 us (8%)
  local copies, waits for them, and re-layouts  6.53 us (5%)
  between operations  1.76 us (1%)
    pallas_call x21, Pallas kernels, call(): pl.pallas_call(kernel, grid_spec=pltpu.PrefetchScalarGridSpec(num_scalar_...  81 us
    ppermute x38, starting transfers between devices, swap(): return lax.ppermute(array, axis, [(i, i ^ bits) for i in range(size)])  34.4 us
    ppermute x38, waiting for transfers between devices, swap(): return lax.ppermute(array, axis, [(i, i ^ bits) for i in range(size)])  11.8 us
    unnamed x48, local copies, waits for them, and re-layouts  6.53 us
    pallas_call x2, Pallas kernels, join(): pl.pallas_call(functools.partial(join_kernel if onehot is None else join_...  5.33 us
  transfers between devices with their start and end apart: 38, of which 8 were waited for; matrix products, arithmetic and copies ran while one was open for 0% of the time, Pallas kernels for 61%

profile of v2, /device:TPU:0, one launch (start us, length us, event | category | flops | bytes accessed | tf_op | source)
XLA Modules:
  0.0 143.2 jit_solution(2617245981761799676)
XLA Ops:
  0.6 3.0 %collective-permute-start = (bf16[192,768]{1,0:T(8,128)(2,1)}, bf16[192,768]{1,0:T(8,128)(2,1)S(1)}, u32[]{:S(2)}, u32[]{:S(2)}) collective-permute-start(bf16[192,768]{1,0:T(8,128)(2,1)} %o0.5), channel_id=1, source_target_pairs={{0,2},{1,3},{2,0},{3,1},{4,6},{5,7},{6,4},{7,5},{8,10},{9,11},{10,... | collective-permute-start | bytes 884744 | tf_op jit(solution)/shard_map/ppermute | solution.py:825
  4.4 1.4 copy-done.1
  10.9 3.3 %project.1 = (bf16[1024,768]{1,0:T(8,128)(2,1)S(1)}, bf16[1024,384]{1,0:T(8,128)(2,1)S(1)}, bf16[1024,384]{1,0:T(8,128)(2,1)S(1)}, bf16[1024,384]{1,0:T(8,128)(2,1)S(1)}) custom-call(s32[10]{0:T(128)S(1)} %pad_add_fusion.ids.refs_0_, bf16[1024,768]{1,0:T(8,128)(2,1)S(1)} %copy-done.1, s32[8,1024]{1,0:T(8,128)S(1)} %bitcast.21, bf16[8,768]{1,0:T(8,128)(2,1)S(1)} %bitcast.26, ...), custom_call_target="tpu_custom_call" | custom-call | flops 8049999872 | bytes 1 | tf_op jit(solution)/shard_map/project/pallas_call | solution.py:62
  15.4 10.2 %attend_first.1 = (bf16[3,1024,512]{2,1,0:T(8,128)(2,1)S(1)}, bf16[192,256]{1,0:T(8,128)(2,1)S(1)}, bf16[192,256]{1,0:T(8,128)(2,1)S(1)}, f32[3,512]{1,0:T(4,128...) custom-call(s32[10]{0:T(128)S(1)} %pad_add_fusion.ids.refs_0_, ...), custom_call_target="tpu_custom_call" | custom-call | flops 16099999744 | bytes 1 | tf_op jit(solution)/shard_map/attend_first/pallas_call | solution.py:62
  27.2 10.0 %attend_last.1 = (bf16[3,1024,512]{2,1,0:T(8,128)(2,1)S(1)}, bf16[192,256]{1,0:T(8,128)(2,1)S(1)}, bf16[192,256]{1,0:T(8,128)(2,1)S(1)}, f32[3,512]{1,0:T(4,128)S(1)}, f32[192,512]{1,0:T(8,128)S(1)}) custom-call(s32[10]{0:T(128)S(1)} %pad_add_fusion.ids.refs_0_, bf16[1024,384]{1,0:T(8,128)(2,1)S(1)} %get-tuple-element.121.refs_1_.refs_7_, ...), custom_call_target="tpu_custom_call" | custom-call | flops 16099999744 | bytes 1 | tf_op jit(solution)/shard_map/attend_last/pallas_call | solution.py:62
  38.2 1.9 %collective-permute-start.9 = (bf16[192,256]{1,0:T(8,128)(2,1)S(1)}, bf16[192,256]{1,0:T(8,128)(2,1)S(1)}, u32[]{:S(2)}, u32[]{:S(2)}) collective-permute-start(bf16[192,256]{1,0:T(8,128)(2,1)S(1)} %get-tuple-element.140.a0.a2), channel_id=1, source_target_pairs={{0,2},{1,3},{2,0},{3,1},{4,6},{5,7},{6,4},{7,5},{8,10},{9,11},{10,... | collective-permute-start | bytes 294920 | tf_op jit(solution)/shard_map/ppermute | solution.py:825
  40.2 4.6 %feed_other.1 = (bf16[2,256,768]{2,1,0:T(8,128)(2,1)S(1)}, bf16[3,256,768]{2,1,0:T(8,128)(2,1)S(1)}, f32[256,768]{1,0:T(8,128)S(1)}, bf16[256,768]{1,0:T(8,128)(2,1)S(1)}, bf16[256,768]{1,0:T(8,128)(2,1)S(1)}) custom-call(s32[10]{0:T(128)S(1)} %pad_add_fusion.ids.refs_0_, bf16[1024,768]{1,0:T(8,128)(2,1)S(1)} %copy-done.2, s32[8,1024]{1,0:T(8,128)S(1)} %bitcast.22, ...), custom_call_target="tpu_custom_call" | custom-call | flops 11500000256 | bytes 1 | tf_op jit(solution)/shard_map/feed_other/pallas_call | solution.py:62
  45.2 4.6 %feed_own.1 = (bf16[2,256,768]{2,1,0:T(8,128)(2,1)S(1)}, bf16[3,256,768]{2,1,0:T(8,128)(2,1)S(1)}, f32[256,768]{1,0:T(8,128)S(1)}, bf16[256,768]{1,0:T(8,128)(2,1)S(1)}, f32[256,768]{1,0:T(8,128)S(1)}) custom-call(s32[10]{0:T(128)S(1)} %pad_add_fusion.ids.refs_0_, bf16[1024,768]{1,0:T(8,128)(2,1)S(1)} %copy-done.2, s32[8,1024]{1,0:T(8,128)S(1)} %bitcast.23, ...), custom_call_target="tpu_custom_call" | custom-call | flops 23000000512 | bytes 1 | tf_op jit(solution)/shard_map/feed_own/pallas_call | solution.py:62
  49.8 1.8 %collective-permute-start.14 = (bf16[256,768]{1,0:T(8,128)(2,1)S(1)}, bf16[256,768]{1,0:T(8,128)(2,1)S(1)}, u32[]{:S(2)}, u32[]{:S(2)}) collective-permute-start(bf16[256,768]{1,0:T(8,128)(2,1)S(1)} %get-tuple-element.145.one_ref), channel_id=1, source_target_pairs={{0,2},{1,3},{2,0},{3,1},{4,6},{5,7},{6,4},{7,5},{8,10},{9,11},{10,... | collective-permute-start | bytes 1179656 | tf_op jit(solution)/shard_map/ppermute | solution.py:825
  51.6 5.2 %collective-permute-done.11.two_ref = bf16[256,768]{1,0:T(8,128)(2,1)S(1)} collective-permute-done((bf16[256,768]{1,0:T(8,128)(2,1)S(1)}, bf16[256,768]{1,0:T(8,128)(2,1)S(1)}, u32[]{:S(2)}, u32[]{:S(2)}) %collective-permute-start.11) | collective-permute-done | bytes 393248 | tf_op jit(solution)/shard_map/ppermute | solution.py:825
  57.4 3.4 %feed_grad.1 = (f32[4,96,1536]{2,1,0:T(8,128)S(1)}, bf16[4,96,1536]{2,1,0:T(8,128)(2,1)S(1)}) custom-call(s32[10]{0:T(128)S(1)} %pad_add_fusion.ids.refs_0_, bf16[2,256,768]{2,1,0:T(8,128)(2,1)S(1)} %get-tuple-element.148.k0, bf16[3,256,768]{2,1,0:T(8,128)(2,1)S(1)} %get-tuple-element.152.n0, bf16[2,256,768]{2,1,0:T(8,128)(2,1)S(1)} %get-tuple-element.150.k1, ...), custom_call_target="tpu_custom_call" | custom-call | flops 8049999872 | bytes 1 | tf_op jit(solution)/shard_map/feed_grad/pallas_call | solution.py:62
  60.9 1.6 %collective-permute-start.21 = (bf16[4,96,1536]{2,1,0:T(8,128)(2,1)S(1)}, bf16[4,96,1536]{2,1,0:T(8,128)(2,1)S(1)}, u32[]{:S(2)}, u32[]{:S(2)}) collective-permute-start(bf16[4,96,1536]{2,1,0:T(8,128)(2,1)S(1)} %get-tuple-element.183), channel_id=1, source_target_pairs={{0,4},{4,0},{8,12},{12,8},{16,20},{20,16},{24,28},{28,24},{1,5},{5... | collective-permute-start | bytes 3538952 | tf_op jit(solution)/shard_map/ppermute | solution.py:825
  65.1 1.8 %mid.1 = (f32[256,768]{1,0:T(8,128)S(1)}, bf16[192,512]{1,0:T(8,128)(2,1)S(1)}, bf16[192,512]{1,0:T(8,128)(2,1)S(1)}, bf16[256,768]{1,0:T(8,128)(2,1)S(1)}, bf16...) custom-call(s32[10]{0:T(128)S(1)} %pad_add_fusion.ids.refs_0_, f32[256,768]{1,0:T(8,128)S(1)} %add.24.own_grad, ...), custom_call_target="tpu_custom_call" | custom-call | flops 11500000 | bytes 1 | tf_op jit(solution)/shard_map/mid/pallas_call | solution.py:62
  67.5 4.5 %back_first.1 = (bf16[3,1024,512]{2,1,0:T(8,128)(2,1)S(1)}, bf16[192,256]{1,0:T(8,128)(2,1)S(1)}, bf16[192,256]{1,0:T(8,128)(2,1)S(1)}, f32[1024,384]{1,0:T(8,12...) custom-call(s32[10]{0:T(128)S(1)} %pad_add_fusion.ids.refs_0_, ...), custom_call_target="tpu_custom_call" | custom-call | flops 2300000000 | bytes 1 | tf_op jit(solution)/shard_map/back_first/pallas_call | solution.py:62
  72.1 4.9 %back_last.1 = (bf16[3,1024,512]{2,1,0:T(8,128)(2,1)S(1)}, bf16[4,3,192,256]{3,2,1,0:T(8,128)(2,1)S(1)}, f32[3,320,128]{2,1,0:T(8,128)S(1)}, f32[3,16,128]{2,1,0:T(8,128)S(1)}) custom-call(s32[10]{0:T(128)S(1)} %pad_add_fusion.ids.refs_0_, bf16[3,1024,512]{2,1,0:T(8,128)(2,1)S(1)} %get-tuple-element.124.refs_1_, ...), custom_call_target="tpu_custom_call" | custom-call | flops 11500000 | bytes 1 | tf_op jit(solution)/shard_map/back_last/pallas_call | solution.py:62
  79.0 2.2 %head_grad.1 = (f32[4,96,768]{2,1,0:T(8,128)S(1)}, bf16[4,96,768]{2,1,0:T(8,128)(2,1)S(1)}) custom-call(s32[10]{0:T(128)S(1)} %pad_add_fusion.ids.refs_0_, bf16[1024,768]{1,0:T(8,128)(2,1)S(1)} %get-tuple-element.126.normed_ref, bf16[4,3,192,256]{3,2,1,0:T(8,128)(2,1)S(1)} %get-tuple-element.176.grads_ref, bf16[256,768]{1,0:T(8,128)(2,1)S(1)} %get-tuple-element.173.l0, ...), custom_call_target="tpu_custom_call" | custom-call | flops 11500000 | bytes 1 | tf_op jit(solution)/shard_map/head_grad/pallas_call | solution.py:62
  82.6 1.8 %collective-permute-start.22 = (bf16[256,768]{1,0:T(8,128)(2,1)S(1)}, bf16[256,768]{1,0:T(8,128)(2,1)S(1)}, u32[]{:S(2)}, u32[]{:S(2)}) collective-permute-start(bf16[256,768]{1,0:T(8,128)(2,1)S(1)} %get-tuple-element.186), channel_id=1, source_target_pairs={{0,2},{1,3},{2,0},{3,1},{4,6},{5,7},{6,4},{7,5},{8,10},{9,11},{10,... | collective-permute-start | bytes 1179656 | tf_op jit(solution)/shard_map/ppermute | solution.py:825
  84.4 5.8 %table_grads.3.hor_a = f32[1,8,32]{2,1,0:T(8,128)S(1)} custom-call(s32[10]{0:T(128)S(1)} %pad_add_fusion.ids.refs_0_, bf16[3,1024,512]{2,1,0:T(8,128)(2,1)S(1)} %get-tuple-element.179.s_ref, bf16[2,1024,1024]{2,1,0:T(8,128)(2,1)S(1)} %get-tuple-element.155.e_ref, s32[2,1024]{1,0:T(2,128)S(1)} %get-tuple-element.197.q_ref), custom_call_target="tpu_custom_call" | custom-call | flops 11500000 | bytes 1 | tf_op jit(solution)/shard_map/table_grads/pallas_call | solution.py:62
  91.0 1.6 %collective-permute-start.25 = (bf16[4,96,768]{2,1,0:T(8,128)(2,1)S(1)}, bf16[4,96,768]{2,1,0:T(8,128)(2,1)S(1)}, u32[]{:S(2)}, u32[]{:S(2)}) collective-permute-start(bf16[4,96,768]{2,1,0:T(8,128)(2,1)S(1)} %get-tuple-element.196), channel_id=1, source_target_pairs={{0,4},{4,0},{8,12},{12,8},{16,20},{20,16},{24,28},{28,24},{1,5},{5... | collective-permute-start | bytes 1769480 | tf_op jit(solution)/shard_map/ppermute | solution.py:825
  92.6 1.6 %collective-permute-start.26 = (bf16[96,1536]{1,0:T(8,128)(2,1)S(1)}, bf16[96,1536]{1,0:T(8,128)(2,1)S(1)}, u32[]{:S(2)}, u32[]{:S(2)}) collective-permute-start(bf16[96,1536]{1,0:T(8,128)(2,1)S(1)} %get-tuple-element.201), channel_id=1, source_target_pairs={{0,8},{4,12},{8,0},{12,4},{16,24},{20,28},{24,16},{28,20},{1,9},{5... | collective-permute-start | bytes 884744 | tf_op jit(solution)/shard_map/ppermute | solution.py:825
  94.2 2.6 %collective-permute-start.27 = (bf16[96,1536]{1,0:T(8,128)(2,1)S(1)}, bf16[96,1536]{1,0:T(8,128)(2,1)S(1)}, u32[]{:S(2)}, u32[]{:S(2)}) collective-permute-start(bf16[96,1536]{1,0:T(8,128)(2,1)S(1)} %get-tuple-element.202), channel_id=1, source_target_pairs={{0,16},{4,20},{8,24},{12,28},{16,0},{20,4},{24,8},{28,12},{1,17},{... | collective-permute-start | bytes 884744 | tf_op jit(solution)/shard_map/ppermute | solution.py:825
  97.0 1.4 last.1
  100.1 5.8 %table_grads.4.ver_a = f32[1,8,32]{2,1,0:T(8,128)S(1)} custom-call(s32[10]{0:T(128)S(1)} %pad_add_fusion.ids.refs_0_, bf16[3,1024,512]{2,1,0:T(8,128)(2,1)S(1)} %get-tuple-element.179.s_ref, bf16[2,1024,1024]{2,1,0:T(8,128)(2,1)S(1)} %get-tuple-element.155.e_ref, s32[2,1024]{1,0:T(2,128)S(1)} %get-tuple-element.197.q_ref), custom_call_target="tpu_custom_call" | custom-call | flops 11500000 | bytes 1 | tf_op jit(solution)/shard_map/table_grads/pallas_call | solution.py:62
  107.6 11.8 %table_grads.5.late = f32[3,8,32]{2,1,0:T(8,128)S(1)} custom-call(s32[10]{0:T(128)S(1)} %pad_add_fusion.ids.refs_0_, bf16[3,1024,512]{2,1,0:T(8,128)(2,1)S(1)} %get-tuple-element.194.s_ref, bf16[2,1024,1024]{2,1,0:T(8,128)(2,1)S(1)} %get-tuple-element.155.e_ref, s32[2,1024]{1,0:T(2,128)S(1)} %get-tuple-element.197.q_ref, ...), custom_call_target="tpu_custom_call" | custom-call | flops 11500000 | bytes 1 | tf_op jit(solution)/shard_map/table_grads/pallas_call | solution.py:62
  122.9 2.4 %collective-permute-start.33 = (bf16[96,768]{1,0:T(8,128)(2,1)S(1)}, bf16[96,768]{1,0:T(8,128)(2,1)S(1)}, u32[]{:S(2)}, u32[]{:S(2)}) collective-permute-start(bf16[96,768]{1,0:T(8,128)(2,1)S(1)} %get-tuple-element.214), channel_id=1, source_target_pairs={{0,8},{4,12},{8,0},{12,4},{16,24},{20,28},{24,16},{28,20},{1,9},{5... | collective-permute-start | bytes 442376 | tf_op jit(solution)/shard_map/ppermute | solution.py:825
  125.3 1.9 %collective-permute-start.34 = (bf16[96,768]{1,0:T(8,128)(2,1)S(1)}, bf16[96,768]{1,0:T(8,128)(2,1)S(1)}, u32[]{:S(2)}, u32[]{:S(2)}) collective-permute-start(bf16[96,768]{1,0:T(8,128)(2,1)S(1)} %get-tuple-element.215), channel_id=1, source_target_pairs={{0,16},{4,20},{8,24},{12,28},{16,0},{20,4},{24,8},{28,12},{1,17},{... | collective-permute-start | bytes 442376 | tf_op jit(solution)/shard_map/ppermute | solution.py:825
  127.2 1.5 %collective-permute-start.35 = (bf16[96,768]{1,0:T(8,128)(2,1)S(1)}, bf16[96,768]{1,0:T(8,128)(2,1)S(1)}, u32[]{:S(2)}, u32[]{:S(2)}) collective-permute-start(bf16[96,768]{1,0:T(8,128)(2,1)S(1)} %get-tuple-element.216), channel_id=1, source_target_pairs={{0,24},{4,28},{8,16},{12,20},{16,8},{20,12},{24,0},{28,4},{1,25},{... | collective-permute-start | bytes 442376 | tf_op jit(solution)/shard_map/ppermute | solution.py:825
  129.3 2.3 %join_output.1 = bf16[1024,768]{1,0:T(8,128)(2,1)} custom-call(s32[10]{0:T(128)S(1)} %pad_add_fusion.ids.refs_0_, bf16[2,256,768]{2,1,0:T(8,128)(2,1)S(1)} %get-tuple-element.210.b0, bf16[2,256,768]{2,1,0:T(8,128)(2,1)S(1)} %collective-permute-done.30.b1, bf16[2,256,768]{2,1,0:T(8,128)(2,1)S(1)} %collective-permute-done.31.b2, ...), custom_call_target="tpu_custom_call" | custom-call | flops 11500000 | bytes 1 | tf_op jit(solution)/shard_map/join_output/pallas_call | solution.py:674
  131.6 3.1 %join_grads.1 = (f32[1024,768]{1,0:T(8,128)}, f32[8,768]{1,0:T(8,128)}) custom-call(s32[10]{0:T(128)S(1)} %pad_add_fusion.ids.refs_0_, bf16[2,256,768]{2,1,0:T(8,128)(2,1)S(1)} %get-tuple-element.210.b0, bf16[2,256,768]{2,1,0:T(8,128)(2,1)S(1)} %collective-permute-done.30.b1, bf16[2,256,768]{2,1,0:T(8,128)(2,1)S(1)} %collective-permute-done.31.b2, ...), custom_call_target="tpu_custom_call" | custom-call | flops 11500000 | bytes 1 | tf_op jit(solution)/shard_map/join_grads/pallas_call | solution.py:674
  135.4 3.5 %collective-permute-start.37 = (f32[24,128]{1,0:T(8,128)S(1)}, f32[24,128]{1,0:T(8,128)S(1)}, u32[]{:S(2)}, u32[]{:S(2)}) collective-permute-start(f32[24,128]{1,0:T(8,128)S(1)} %add.16.one_ref), channel_id=1, source_target_pairs={{0,16},{4,20},{8,24},{12,28},{16,0},{20,4},{24,8},{28,12},{1,17},{... | collective-permute-start | bytes 36872 | tf_op jit(solution)/shard_map/ppermute | solution.py:825
  139.2 2.6 %collective-permute-done.37.two_ref = f32[24,128]{1,0:T(8,128)S(1)} collective-permute-done((f32[24,128]{1,0:T(8,128)S(1)}, f32[24,128]{1,0:T(8,128)S(1)}, u32[]{:S(2)}, u32[]{:S(2)}) %collective-permute-start.37) | collective-permute-done | bytes 12320 | tf_op jit(solution)/shard_map/ppermute | solution.py:825
  141.8 1.4 head_final.1
  (122 shorter events, 26.0 us)
Async XLA Ops:
  0.6 14.3 %collective-permute-start = (bf16[192,768]{1,0:T(8,128)(2,1)}, bf16[192,768]{1,0:T(8,128)(2,1)S(1)}, u32[]{:S(2)}, u32[]{:S(2)}) collective-permute-start(bf16[192,768]{1,0:T(8,128)(2,1)} %o0.5), channel_id=1, source_target_pairs={{0,2},{1,3},{2,0},{3,1},{4,6},{5,7},{6,4},{7,5},{8,10},{9,11},{10,... | collective-permute-start | bytes 884744 | tf_op jit(solution)/shard_map/ppermute | solution.py:825
  3.7 36.4 %collective-permute-start.7 = (bf16[192,768]{1,0:T(8,128)(2,1)}, bf16[192,768]{1,0:T(8,128)(2,1)S(1)}, u32[]{:S(2)}, u32[]{:S(2)}) collective-permute-start(bf16[192,768]{1,0:T(8,128)(2,1)} %o0.5), channel_id=1, source_target_pairs={{0,1},{1,0},{2,3},{3,2},{4,5},{5,4},{6,7},{7,6},{8,9},{9,8},{10,11... | collective-permute-start | bytes 884744 | tf_op jit(solution)/shard_map/ppermute | solution.py:825
  14.3 12.9 %collective-permute-start.2 = (bf16[768,768]{1,0:T(8,128)(2,1)S(1)}, bf16[768,768]{1,0:T(8,128)(2,1)S(1)}, u32[]{:S(2)}, u32[]{:S(2)}) collective-permute-start(bf16[768,768]{1,0:T(8,128)(2,1)S(1)} %copy-done.17), channel_id=1, source_target_pairs={{0,1},{1,0},{2,3},{3,2},{4,5},{5,4},{6,7},{7,6},{8,9},{9,8},{10,11... | collective-permute-start | bytes 3538952 | tf_op jit(solution)/shard_map/ppermute | solution.py:825
  14.8 12.3 %collective-permute-start.3 = (bf16[768,768]{1,0:T(8,128)(2,1)S(1)}, bf16[768,768]{1,0:T(8,128)(2,1)S(1)}, u32[]{:S(2)}, u32[]{:S(2)}) collective-permute-start(bf16[768,768]{1,0:T(8,128)(2,1)S(1)} %copy-done.18), channel_id=1, source_target_pairs={{0,1},{1,0},{2,3},{3,2},{4,5},{5,4},{6,7},{7,6},{8,9},{9,8},{10,11... | collective-permute-start | bytes 3538952 | tf_op jit(solution)/shard_map/ppermute | solution.py:825
  14.9 10.8 %collective-permute-start.1 = (bf16[192,768]{1,0:T(8,128)(2,1)S(1)}, bf16[192,768]{1,0:T(8,128)(2,1)S(1)}, u32[]{:S(2)}, u32[]{:S(2)}) collective-permute-start(bf16[192,768]{1,0:T(8,128)(2,1)S(1)} %collective-permute-done.o2), channel_id=1, source_target_pairs={{0,1},{1,0},{2,3},{3,2},{4,5},{5,4},{6,7},{7,6},{8,9},{9,8},{10,11... | collective-permute-start | bytes 884744 | tf_op jit(solution)/shard_map/ppermute | solution.py:825
  25.6 12.4 %collective-permute-start.5 = (bf16[192,256]{1,0:T(8,128)(2,1)S(1)}, bf16[192,256]{1,0:T(8,128)(2,1)S(1)}, u32[]{:S(2)}, u32[]{:S(2)}) collective-permute-start(bf16[192,256]{1,0:T(8,128)(2,1)S(1)} %get-tuple-element.144.a0), channel_id=1, source_target_pairs={{0,2},{1,3},{2,0},{3,1},{4,6},{5,7},{6,4},{7,5},{8,10},{9,11},{10,... | collective-permute-start | bytes 294920 | tf_op jit(solution)/shard_map/ppermute | solution.py:825
  25.7 12.4 %collective-permute-start.6 = (bf16[192,256]{1,0:T(8,128)(2,1)S(1)}, bf16[192,256]{1,0:T(8,128)(2,1)S(1)}, u32[]{:S(2)}, u32[]{:S(2)}) collective-permute-start(bf16[192,256]{1,0:T(8,128)(2,1)S(1)} %get-tuple-element.142.a1), channel_id=1, source_target_pairs={{0,3},{1,2},{2,1},{3,0},{4,7},{5,6},{6,5},{7,4},{8,11},{9,10},{10,... | collective-permute-start | bytes 294920 | tf_op jit(solution)/shard_map/ppermute | solution.py:825
  37.9 7.1 %collective-permute-start.8 = (bf16[192,256]{1,0:T(8,128)(2,1)S(1)}, bf16[192,256]{1,0:T(8,128)(2,1)S(1)}, u32[]{:S(2)}, u32[]{:S(2)}) collective-permute-start(bf16[192,256]{1,0:T(8,128)(2,1)S(1)} %get-tuple-element.142.a1), channel_id=1, source_target_pairs={{0,1},{1,0},{2,3},{3,2},{4,5},{5,4},{6,7},{7,6},{8,9},{9,8},{10,11... | collective-permute-start | bytes 294920 | tf_op jit(solution)/shard_map/ppermute | solution.py:825
  38.0 7.0 %collective-permute-start.10 = (bf16[192,256]{1,0:T(8,128)(2,1)S(1)}, bf16[192,256]{1,0:T(8,128)(2,1)S(1)}, u32[]{:S(2)}, u32[]{:S(2)}) collective-permute-start(bf16[192,256]{1,0:T(8,128)(2,1)S(1)} %get-tuple-element.141.a3), channel_id=1, source_target_pairs={{0,3},{1,2},{2,1},{3,0},{4,7},{5,6},{6,5},{7,4},{8,11},{9,10},{10,... | collective-permute-start | bytes 294920 | tf_op jit(solution)/shard_map/ppermute | solution.py:825
  38.2 7.1 %collective-permute-start.9 = (bf16[192,256]{1,0:T(8,128)(2,1)S(1)}, bf16[192,256]{1,0:T(8,128)(2,1)S(1)}, u32[]{:S(2)}, u32[]{:S(2)}) collective-permute-start(bf16[192,256]{1,0:T(8,128)(2,1)S(1)} %get-tuple-element.140.a0.a2), channel_id=1, source_target_pairs={{0,2},{1,3},{2,0},{3,1},{4,6},{5,7},{6,4},{7,5},{8,10},{9,11},{10,... | collective-permute-start | bytes 294920 | tf_op jit(solution)/shard_map/ppermute | solution.py:825
  44.7 6.8 %collective-permute-start.12 = (bf16[3,256,768]{2,1,0:T(8,128)(2,1)S(1)}, bf16[3,256,768]{2,1,0:T(8,128)(2,1)S(1)}, u32[]{:S(2)}, u32[]{:S(2)}) collective-permute-start(bf16[3,256,768]{2,1,0:T(8,128)(2,1)S(1)} %get-tuple-element.151.n1), channel_id=1, source_target_pairs={{0,1},{1,0},{2,3},{3,2},{4,5},{5,4},{6,7},{7,6},{8,9},{9,8},{10,11... | collective-permute-start | bytes 3538952 | tf_op jit(solution)/shard_map/ppermute | solution.py:825
  44.8 12.0 %collective-permute-start.11 = (bf16[256,768]{1,0:T(8,128)(2,1)S(1)}, bf16[256,768]{1,0:T(8,128)(2,1)S(1)}, u32[]{:S(2)}, u32[]{:S(2)}) collective-permute-start(bf16[256,768]{1,0:T(8,128)(2,1)S(1)} %get-tuple-element.146.other_grad), channel_id=1, source_target_pairs={{0,2},{1,3},{2,0},{3,1},{4,6},{5,7},{6,4},{7,5},{8,10},{9,11},{10,... | collective-permute-start | bytes 1179656 | tf_op jit(solution)/shard_map/ppermute | solution.py:825
  49.8 15.0 %collective-permute-start.14 = (bf16[256,768]{1,0:T(8,128)(2,1)S(1)}, bf16[256,768]{1,0:T(8,128)(2,1)S(1)}, u32[]{:S(2)}, u32[]{:S(2)}) collective-permute-start(bf16[256,768]{1,0:T(8,128)(2,1)S(1)} %get-tuple-element.145.one_ref), channel_id=1, source_target_pairs={{0,2},{1,3},{2,0},{3,1},{4,6},{5,7},{6,4},{7,5},{8,10},{9,11},{10,... | collective-permute-start | bytes 1179656 | tf_op jit(solution)/shard_map/ppermute | solution.py:825
  51.6 5.9 %collective-permute-start.13 = (bf16[3,256,768]{2,1,0:T(8,128)(2,1)S(1)}, bf16[3,256,768]{2,1,0:T(8,128)(2,1)S(1)}, u32[]{:S(2)}, u32[]{:S(2)}) collective-permute-start(bf16[3,256,768]{2,1,0:T(8,128)(2,1)S(1)} %get-tuple-element.152.n0), channel_id=1, source_target_pairs={{0,1},{1,0},{2,3},{3,2},{4,5},{5,4},{6,7},{7,6},{8,9},{9,8},{10,11... | collective-permute-start | bytes 3538952 | tf_op jit(solution)/shard_map/ppermute | solution.py:825
  60.9 29.4 %collective-permute-start.21 = (bf16[4,96,1536]{2,1,0:T(8,128)(2,1)S(1)}, bf16[4,96,1536]{2,1,0:T(8,128)(2,1)S(1)}, u32[]{:S(2)}, u32[]{:S(2)}) collective-permute-start(bf16[4,96,1536]{2,1,0:T(8,128)(2,1)S(1)} %get-tuple-element.183), channel_id=1, source_target_pairs={{0,4},{4,0},{8,12},{12,8},{16,20},{20,16},{24,28},{28,24},{1,5},{5... | collective-permute-start | bytes 3538952 | tf_op jit(solution)/shard_map/ppermute | solution.py:825
  64.8 12.2 %collective-permute-start.16 = (bf16[256,768]{1,0:T(8,128)(2,1)S(1)}, bf16[256,768]{1,0:T(8,128)(2,1)S(1)}, u32[]{:S(2)}, u32[]{:S(2)}) collective-permute-start(bf16[256,768]{1,0:T(8,128)(2,1)S(1)} %get-tuple-element.169), channel_id=1, source_target_pairs={{0,2},{1,3},{2,0},{3,1},{4,6},{5,7},{6,4},{7,5},{8,10},{9,11},{10,... | collective-permute-start | bytes 1179656 | tf_op jit(solution)/shard_map/ppermute | solution.py:825
  66.9 12.0 %collective-permute-start.17 = (bf16[256,768]{1,0:T(8,128)(2,1)S(1)}, bf16[256,768]{1,0:T(8,128)(2,1)S(1)}, u32[]{:S(2)}, u32[]{:S(2)}) collective-permute-start(bf16[256,768]{1,0:T(8,128)(2,1)S(1)} %get-tuple-element.173.l0), channel_id=1, source_target_pairs={{0,1},{1,0},{2,3},{3,2},{4,5},{5,4},{6,7},{7,6},{8,9},{9,8},{10,11... | collective-permute-start | bytes 1179656 | tf_op jit(solution)/shard_map/ppermute | solution.py:825
  67.4 11.5 %collective-permute-start.18 = (bf16[256,768]{1,0:T(8,128)(2,1)S(1)}, bf16[256,768]{1,0:T(8,128)(2,1)S(1)}, u32[]{:S(2)}, u32[]{:S(2)}) collective-permute-start(bf16[256,768]{1,0:T(8,128)(2,1)S(1)} %get-tuple-element.174.l2), channel_id=1, source_target_pairs={{0,1},{1,0},{2,3},{3,2},{4,5},{5,4},{6,7},{7,6},{8,9},{9,8},{10,11... | collective-permute-start | bytes 1179656 | tf_op jit(solution)/shard_map/ppermute | solution.py:825
  82.6 14.4 %collective-permute-start.22 = (bf16[256,768]{1,0:T(8,128)(2,1)S(1)}, bf16[256,768]{1,0:T(8,128)(2,1)S(1)}, u32[]{:S(2)}, u32[]{:S(2)}) collective-permute-start(bf16[256,768]{1,0:T(8,128)(2,1)S(1)} %get-tuple-element.186), channel_id=1, source_target_pairs={{0,2},{1,3},{2,0},{3,1},{4,6},{5,7},{6,4},{7,5},{8,10},{9,11},{10,... | collective-permute-start | bytes 1179656 | tf_op jit(solution)/shard_map/ppermute | solution.py:825
  91.0 15.5 %collective-permute-start.25 = (bf16[4,96,768]{2,1,0:T(8,128)(2,1)S(1)}, bf16[4,96,768]{2,1,0:T(8,128)(2,1)S(1)}, u32[]{:S(2)}, u32[]{:S(2)}) collective-permute-start(bf16[4,96,768]{2,1,0:T(8,128)(2,1)S(1)} %get-tuple-element.196), channel_id=1, source_target_pairs={{0,4},{4,0},{8,12},{12,8},{16,20},{20,16},{24,28},{28,24},{1,5},{5... | collective-permute-start | bytes 1769480 | tf_op jit(solution)/shard_map/ppermute | solution.py:825
  92.6 27.4 %collective-permute-start.26 = (bf16[96,1536]{1,0:T(8,128)(2,1)S(1)}, bf16[96,1536]{1,0:T(8,128)(2,1)S(1)}, u32[]{:S(2)}, u32[]{:S(2)}) collective-permute-start(bf16[96,1536]{1,0:T(8,128)(2,1)S(1)} %get-tuple-element.201), channel_id=1, source_target_pairs={{0,8},{4,12},{8,0},{12,4},{16,24},{20,28},{24,16},{28,20},{1,9},{5... | collective-permute-start | bytes 884744 | tf_op jit(solution)/shard_map/ppermute | solution.py:825
  94.2 25.8 %collective-permute-start.27 = (bf16[96,1536]{1,0:T(8,128)(2,1)S(1)}, bf16[96,1536]{1,0:T(8,128)(2,1)S(1)}, u32[]{:S(2)}, u32[]{:S(2)}) collective-permute-start(bf16[96,1536]{1,0:T(8,128)(2,1)S(1)} %get-tuple-element.202), channel_id=1, source_target_pairs={{0,16},{4,20},{8,24},{12,28},{16,0},{20,4},{24,8},{28,12},{1,17},{... | collective-permute-start | bytes 884744 | tf_op jit(solution)/shard_map/ppermute | solution.py:825
  96.7 23.3 %collective-permute-start.28 = (bf16[96,1536]{1,0:T(8,128)(2,1)S(1)}, bf16[96,1536]{1,0:T(8,128)(2,1)S(1)}, u32[]{:S(2)}, u32[]{:S(2)}) collective-permute-start(bf16[96,1536]{1,0:T(8,128)(2,1)S(1)} %get-tuple-element.203), channel_id=1, source_target_pairs={{0,24},{4,28},{8,16},{12,20},{16,8},{20,12},{24,0},{28,4},{1,25},{... | collective-permute-start | bytes 884744 | tf_op jit(solution)/shard_map/ppermute | solution.py:825
  99.6 21.2 %collective-permute-start.31 = (bf16[2,256,768]{2,1,0:T(8,128)(2,1)S(1)}, bf16[2,256,768]{2,1,0:T(8,128)(2,1)S(1)}, u32[]{:S(2)}, u32[]{:S(2)}) collective-permute-start(bf16[2,256,768]{2,1,0:T(8,128)(2,1)S(1)} %get-tuple-element.210.b0), channel_id=1, source_target_pairs={{0,2},{1,3},{2,0},{3,1},{4,6},{5,7},{6,4},{7,5},{8,10},{9,11},{10,... | collective-permute-start | bytes 2359304 | tf_op jit(solution)/shard_map/ppermute | solution.py:825
  106.5 12.9 %collective-permute-start.24 = (f32[2,768]{1,0:T(2,128)S(1)}, f32[2,768]{1,0:T(2,128)S(1)}, u32[]{:S(2)}, u32[]{:S(2)}) collective-permute-start(f32[2,768]{1,0:T(2,128)S(1)} %add.14.gains_ref), channel_id=1, source_target_pairs={{0,2},{1,3},{2,0},{3,1},{4,6},{5,7},{6,4},{7,5},{8,10},{9,11},{10,... | collective-permute-start | bytes 18440 | tf_op jit(solution)/shard_map/ppermute | solution.py:825
  119.4 9.3 %collective-permute-start.30 = (bf16[2,256,768]{2,1,0:T(8,128)(2,1)S(1)}, bf16[2,256,768]{2,1,0:T(8,128)(2,1)S(1)}, u32[]{:S(2)}, u32[]{:S(2)}) collective-permute-start(bf16[2,256,768]{2,1,0:T(8,128)(2,1)S(1)} %get-tuple-element.210.b0), channel_id=1, source_target_pairs={{0,1},{1,0},{2,3},{3,2},{4,5},{5,4},{6,7},{7,6},{8,9},{9,8},{10,11... | collective-permute-start | bytes 2359304 | tf_op jit(solution)/shard_map/ppermute | solution.py:825
  120.9 8.4 %collective-permute-start.32 = (bf16[2,256,768]{2,1,0:T(8,128)(2,1)S(1)}, bf16[2,256,768]{2,1,0:T(8,128)(2,1)S(1)}, u32[]{:S(2)}, u32[]{:S(2)}) collective-permute-start(bf16[2,256,768]{2,1,0:T(8,128)(2,1)S(1)} %collective-permute-done.31.b2), channel_id=1, source_target_pairs={{0,1},{1,0},{2,3},{3,2},{4,5},{5,4},{6,7},{7,6},{8,9},{9,8},{10,11... | collective-permute-start | bytes 2359304 | tf_op jit(solution)/shard_map/ppermute | solution.py:825
  122.9 16.0 %collective-permute-start.33 = (bf16[96,768]{1,0:T(8,128)(2,1)S(1)}, bf16[96,768]{1,0:T(8,128)(2,1)S(1)}, u32[]{:S(2)}, u32[]{:S(2)}) collective-permute-start(bf16[96,768]{1,0:T(8,128)(2,1)S(1)} %get-tuple-element.214), channel_id=1, source_target_pairs={{0,8},{4,12},{8,0},{12,4},{16,24},{20,28},{24,16},{28,20},{1,9},{5... | collective-permute-start | bytes 442376 | tf_op jit(solution)/shard_map/ppermute | solution.py:825
  125.3 13.9 %collective-permute-start.34 = (bf16[96,768]{1,0:T(8,128)(2,1)S(1)}, bf16[96,768]{1,0:T(8,128)(2,1)S(1)}, u32[]{:S(2)}, u32[]{:S(2)}) collective-permute-start(bf16[96,768]{1,0:T(8,128)(2,1)S(1)} %get-tuple-element.215), channel_id=1, source_target_pairs={{0,16},{4,20},{8,24},{12,28},{16,0},{20,4},{24,8},{28,12},{1,17},{... | collective-permute-start | bytes 442376 | tf_op jit(solution)/shard_map/ppermute | solution.py:825
  127.2 12.1 %collective-permute-start.35 = (bf16[96,768]{1,0:T(8,128)(2,1)S(1)}, bf16[96,768]{1,0:T(8,128)(2,1)S(1)}, u32[]{:S(2)}, u32[]{:S(2)}) collective-permute-start(bf16[96,768]{1,0:T(8,128)(2,1)S(1)} %get-tuple-element.216), channel_id=1, source_target_pairs={{0,24},{4,28},{8,16},{12,20},{16,8},{20,12},{24,0},{28,4},{1,25},{... | collective-permute-start | bytes 442376 | tf_op jit(solution)/shard_map/ppermute | solution.py:825
  128.7 6.7 %collective-permute-start.36 = (f32[24,128]{1,0:T(8,128)S(1)}, f32[24,128]{1,0:T(8,128)S(1)}, u32[]{:S(2)}, u32[]{:S(2)}) collective-permute-start(f32[24,128]{1,0:T(8,128)S(1)} %add.15), channel_id=1, source_target_pairs={{0,8},{4,12},{8,0},{12,4},{16,24},{20,28},{24,16},{28,20},{1,9},{5... | collective-permute-start | bytes 36872 | tf_op jit(solution)/shard_map/ppermute | solution.py:825
  135.4 6.4 %collective-permute-start.37 = (f32[24,128]{1,0:T(8,128)S(1)}, f32[24,128]{1,0:T(8,128)S(1)}, u32[]{:S(2)}, u32[]{:S(2)}) collective-permute-start(f32[24,128]{1,0:T(8,128)S(1)} %add.16.one_ref), channel_id=1, source_target_pairs={{0,16},{4,20},{8,24},{12,28},{16,0},{20,4},{24,8},{28,12},{1,17},{... | collective-permute-start | bytes 36872 | tf_op jit(solution)/shard_map/ppermute | solution.py:825
  (30 other events, 155.9 us)
